TPU v7x, 512 devices: a whole 4x4x16 slice. The times are simulated.
512 devices in a mesh: gx: 32 (over z, core), gy: 16 (over y, x).
Axes of the slice: x: 4, y: 4, z: 16, core: 2. Of those that a mesh axis runs over, the one named last changes fastest.
Arguments:
- source: float32 [256, 2048, 256], P('gx', 'gy'), may hold values from -8 to 8
- density: float32 [256, 2048, 256], P('gx', 'gy'), may hold values from 0.08 to 1.7
Outputs:
- pressure: float32 [256, 2048, 256], P('gx', 'gy')
- residual: float32 [256, 2048, 256], P('gx', 'gy')
All inputs are finite; a program needn't handle non-finite values.
Results may differ from a plain program's by a relative error of at most 0.00021.
Values sent between devices are 32-bit elements; how exact they have to be, the bound alone decides.
A program may use at most 64 MiB of HBM per device.

v0:
```python
import jax
import jax.numpy as jnp
from jax import lax
from jax.sharding import PartitionSpec as P

ITERS = 2


def extended(shard, sides, width):
    for axis, dim in sides:
        devices, length = (lax.axis_size(axis), shard.shape[dim])
        up = [(i, (i + 1) % devices) for i in range(devices - 1)]
        down = [(j, i) for i, j in up]
        last = lax.slice_in_dim(shard, length - width, length, axis=dim)
        initial = lax.slice_in_dim(shard, 0, width, axis=dim)
        before = lax.ppermute(last, axis, up)
        after = lax.ppermute(initial, axis, down)
        shard = jnp.concatenate([before, shard, after], axis=dim)
    return shard


def neighbours(padded):
    return [
        padded[2:, 1:-1, 1:-1],
        padded[:-2, 1:-1, 1:-1],
        padded[1:-1, 2:, 1:-1],
        padded[1:-1, :-2, 1:-1],
        padded[1:-1, 1:-1, 2:],
        padded[1:-1, 1:-1, :-2],
    ]


def pad_depth(field):
    return jnp.pad(field, ((0, 0), (0, 0), (1, 1)))


def weights_from(center, padded):
    nearby = neighbours(pad_depth(padded))
    weights = [2.0 / jnp.where(center > 0, center + other, 1.0) for other in nearby]
    diag_sum = weights[0]
    for weight_one in weights[1:]:
        diag_sum = diag_sum + weight_one
    return (weights, lax.rsqrt(diag_sum))


def couple(padded, weights):
    nearby = neighbours(pad_depth(padded))
    total = weights[0] * nearby[0]
    for weight_one, other in zip(weights[1:], nearby[1:]):
        total = total + weight_one * other
    return total


def scaled_apply(field, weights, scale_inv):
    scaled = scale_inv * field
    padded = extended(scaled, (("gx", 0), ("gy", 1)), 1)
    return field - scale_inv * couple(padded, weights)


def inner_pair(residual, shadow):
    gamma_part = jnp.sum(residual * residual)
    delta_part = jnp.sum(shadow * residual)
    return lax.psum((gamma_part, delta_part), ("gx", "gy"))


def shards(source, density):
    rim_density = extended(density, (("gx", 0), ("gy", 1)), 1)
    weights, scale_inv = weights_from(density, rim_density)
    residual = scale_inv * source
    shadow = scaled_apply(residual, weights, scale_inv)
    solution = jnp.zeros_like(source)
    direction = jnp.zeros_like(source)
    along = jnp.zeros_like(source)
    pushed = jnp.zeros_like(source)
    gamma_old = jnp.float32(1.0)
    alpha_old = jnp.float32(1.0)
    for iteration in range(ITERS):
        gamma_now, delta_now = inner_pair(residual, shadow)
        fresh = scaled_apply(shadow, weights, scale_inv)
        if iteration == 0:
            beta_now = jnp.float32(0.0)
            alpha_now = gamma_now / delta_now
        else:
            beta_now = gamma_now / gamma_old
            alpha_now = gamma_now / (delta_now - beta_now * gamma_now / alpha_old)
        pushed = fresh + beta_now * pushed
        along = shadow + beta_now * along
        direction = residual + beta_now * direction
        solution = solution + alpha_now * direction
        residual = residual - alpha_now * along
        shadow = shadow - alpha_now * pushed
        gamma_old = gamma_now
        alpha_old = alpha_now
    return (scale_inv * solution, residual)


def solution(mesh):
    in_specs = (P("gx", "gy", None), P("gx", "gy", None))
    out_specs = (P("gx", "gy", None), P("gx", "gy", None))
    return jax.shard_map(shards, mesh=mesh, in_specs=in_specs, out_specs=out_specs, check_vma=False)
```

profile of v0, /device:TPU:1, one launch (start us, length us, event | category | flops | bytes accessed | tf_op | source)
XLA Modules:
  0.0 292.1 jit_solution(12491736023000275440)
XLA Ops:
  0.6 1.0 fusion.49
  1.6 4.9 %collective-permute-start.1 = (f32[1,128,256]{2,1,0:T(8,128)S(1)}, f32[1,128,256]{2,1,0:T(8,128)S(1)}, u32[]{:S(2)}, u32[]{:S(2)}) collective-permute-start(f32[1,128,256]{2,1,0:T(8,128)S(1)} %get-tuple-element.30), channel_id=1, source_target_pairs={{0,16},{16,32},{32,48},{48,64},{64,80},{80,96},{96,112},{112,128},... | collective-permute-start | bytes 393224 | tf_op jit(solution)/shard_map/ppermute | solution.py:16
  6.6 5.1 %collective-permute-start = (f32[1,128,256]{2,1,0:T(8,128)S(1)}, f32[1,128,256]{2,1,0:T(8,128)S(1)}, u32[]{:S(2)}, u32[]{:S(2)}) collective-permute-start(f32[1,128,256]{2,1,0:T(8,128)S(1)} %get-tuple-element.29), channel_id=1, source_target_pairs={{16,0},{32,16},{48,32},{64,48},{80,64},{96,80},{112,96},{128,112},... | collective-permute-start | bytes 393224 | tf_op jit(solution)/shard_map/ppermute | solution.py:17
  11.7 1.3 constant_dynamic-update-slice_fusion.1
  13.1 2.9 collective-permute-start.3
  16.0 1.3 collective-permute-start.2
  17.3 3.1 %collective-permute-done.2 = f32[10,1,256]{2,1,0:T(1,128)S(1)} collective-permute-done((f32[10,1,256]{2,1,0:T(1,128)S(1)}, f32[10,1,256]{2,1,0:T(1,128)S(1)}, u32[]{:S(2)}, u32[]{:S(2)}) %collective-permute-start.2) | collective-permute-done | bytes 10272 | tf_op jit(solution)/shard_map/ppermute | solution.py:17
  20.4 0.7 select_maximum_fusion.8
  21.2 2.2 fusion.43
  23.4 0.0 copy-start.4
  23.5 3.3 %collective-permute-start.5 = (f32[1,128,256]{2,1,0:T(8,128)S(1)}, f32[1,128,256]{2,1,0:T(8,128)S(1)}, u32[]{:S(2)}, u32[]{:S(2)}) collective-permute-start(f32[1,128,256]{2,1,0:T(8,128)S(1)} %get-tuple-element.27), channel_id=1, source_target_pairs={{0,16},{16,32},{32,48},{48,64},{64,80},{80,96},{96,112},{112,128},... | collective-permute-start | bytes 393224 | tf_op jit(solution)/shard_map/ppermute | solution.py:16
  26.8 1.9 collective-permute-start.4
  28.8 4.3 %collective-permute-done.4 = f32[1,128,256]{2,1,0:T(8,128)S(1)} collective-permute-done((f32[1,128,256]{2,1,0:T(8,128)S(1)}, f32[1,128,256]{2,1,0:T(8,128)S(1)}, u32[]{:S(2)}, u32[]{:S(2)}) %collective-permute-start.4) | collective-permute-done | bytes 131104 | tf_op jit(solution)/shard_map/ppermute | solution.py:17
  33.1 3.1 %collective-permute-start.7 = (f32[10,1,256]{2,1,0:T(1,128)S(1)}, f32[10,1,256]{2,1,0:T(1,128)S(1)}, u32[]{:S(2)}, u32[]{:S(2)}) collective-permute-start(f32[10,1,256]{2,1,0:T(1,128)S(1)} %get-tuple-element.21), channel_id=1, source_target_pairs={{0,1},{1,2},{2,3},{3,4},{4,5},{5,6},{6,7},{7,8},{8,9},{9,10},{10,1... | collective-permute-start | bytes 30728 | tf_op jit(solution)/shard_map/ppermute | solution.py:16
  36.3 1.3 collective-permute-start.6
  37.6 3.1 %collective-permute-done.6 = f32[10,1,256]{2,1,0:T(1,128)S(1)} collective-permute-done((f32[10,1,256]{2,1,0:T(1,128)S(1)}, f32[10,1,256]{2,1,0:T(1,128)S(1)}, u32[]{:S(2)}, u32[]{:S(2)}) %collective-permute-start.6) | collective-permute-done | bytes 10272 | tf_op jit(solution)/shard_map/ppermute | solution.py:17
  40.7 0.7 select_maximum_fusion.4
  41.4 3.4 %multiply_reduce_fusion.2 = (f32[]{:T(128)}, f32[]{:T(128)}, f32[8,128,256]{2,1,0:T(8,128)S(1)}) fusion(f32[8,128,256]{2,1,0:T(8,128)S(1)} %get-tuple-element.13, f32[8,128,256]{2,1,0:T(8,128)S(1)} %get-tuple-element.14, f32[10,130,258]{2,1,0:T(8,128)S(1)} %select_maximum_fusion.4, f32[8,128,256]{2,1,0:T(8,128)S(1)} %copy-done, ...), kind=kLoop, calls=%fused_computation.84 | loop fusion | flops 10485758 | bytes 12079112 | tf_op jit(solution)/shard_map/reduce_sum | solution.py:62
  44.9 0.1 mul.118
  45.1 3.2 %collective-permute-start.9 = (f32[1,128,256]{2,1,0:T(8,128)S(1)}, f32[1,128,256]{2,1,0:T(8,128)S(1)}, u32[]{:S(2)}, u32[]{:S(2)}) collective-permute-start(f32[1,128,256]{2,1,0:T(8,128)S(1)} %get-tuple-element.25), channel_id=1, source_target_pairs={{0,16},{16,32},{32,48},{48,64},{64,80},{80,96},{96,112},{112,128},... | collective-permute-start | bytes 393224 | tf_op jit(solution)/shard_map/ppermute | solution.py:16
  48.3 1.9 collective-permute-start.8
  50.2 4.3 %collective-permute-done.8 = f32[1,128,256]{2,1,0:T(8,128)S(1)} collective-permute-done((f32[1,128,256]{2,1,0:T(8,128)S(1)}, f32[1,128,256]{2,1,0:T(8,128)S(1)}, u32[]{:S(2)}, u32[]{:S(2)}) %collective-permute-start.8) | collective-permute-done | bytes 131104 | tf_op jit(solution)/shard_map/ppermute | solution.py:17
  54.6 0.7 pad_maximum_fusion.20
  55.2 0.0 copy-done.9
  55.2 4.4 %collective-permute-start.11 = (f32[10,1,256]{2,1,0:T(1,128)}, f32[10,1,256]{2,1,0:T(1,128)S(1)}, u32[]{:S(2)}, u32[]{:S(2)}) collective-permute-start(f32[10,1,256]{2,1,0:T(1,128)} %get-tuple-element.19), channel_id=1, source_target_pairs={{0,1},{1,2},{2,3},{3,4},{4,5},{5,6},{6,7},{7,8},{8,9},{9,10},{10,1... | collective-permute-start | bytes 30728 | tf_op jit(solution)/shard_map/ppermute | solution.py:16
  59.6 1.3 collective-permute-start.10
  60.9 114.2 %all-reduce.4 = (f32[]{:T(128)}, f32[]{:T(128)}) all-reduce(f32[]{:T(128)} %get-tuple-element.5, f32[]{:T(128)} %get-tuple-element.4), channel_id=1, replica_groups=mesh['gx'=32,'gy'=16] {'gx','gy'}, use_global_device_ids=true, to_apply=%region_1.2 | all-reduce | flops 2 | bytes 16 | tf_op jit(solution)/shard_map/psum | solution.py:63
  176.4 0.0 copy-start.1
  176.5 2.2 select_maximum_fusion
  178.7 5.7 %multiply_reduce_fusion = (f32[]{:T(128)}, f32[]{:T(128)}, f32[8,128,256]{2,1,0:T(8,128)}) fusion(f32[8,128,256]{2,1,0:T(8,128)S(1)} %copy-done.5, f32[8,128,256]{2,1,0:T(8,128)} %copy-done.6, f32[]{:T(128)S(6)} %div.36, f32[8,128,256]{2,1,0:T(8,128)S(1)} %get-tuple-element.14, f32[10,130,258]{2,1,0:T(8,128)S(1)} %select_maximum_fusion, ...), kind=kLoop, calls=%fused_computation.81 | loop fusion | flops 11534334 | bytes 13127692 | tf_op jit(solution)/shard_map/reduce_sum | solution.py:62
  184.4 99.5 %all-reduce.3 = (f32[]{:T(128)}, f32[]{:T(128)}) all-reduce(f32[]{:T(128)} %get-tuple-element.3, f32[]{:T(128)} %get-tuple-element.2), channel_id=1, replica_groups=mesh['gx'=32,'gy'=16] {'gx','gy'}, use_global_device_ids=true, to_apply=%region_5.6 | all-reduce | flops 2 | bytes 16 | tf_op jit(solution)/shard_map/psum | solution.py:63
  288.5 3.6 %multiply_subtract_fusion = (f32[8,128,256]{2,1,0:T(8,128)}, f32[8,128,256]{2,1,0:T(8,128)}) fusion(f32[8,128,256]{2,1,0:T(8,128)} %get-tuple-element.10, f32[8,128,256]{2,1,0:T(8,128)} %copy-done.6, f32[]{:T(128)S(6)} %div.37, f32[]{:T(128)S(6)} %div.39, f32[8,128,256]{2,1,0:T(8,128)} %copy-done.4, f32[]{:T(128)S(6)} %div.36, ...), kind=kLoop, calls=%fused_computation.79 | loop fusion | flops 3145728 | bytes 6291468 | tf_op jit(solution)/shard_map/sub | solution.py:90
  (35 shorter events, 0.2 us)
Async XLA Ops:
  1.6 10.1 %collective-permute-start.1 = (f32[1,128,256]{2,1,0:T(8,128)S(1)}, f32[1,128,256]{2,1,0:T(8,128)S(1)}, u32[]{:S(2)}, u32[]{:S(2)}) collective-permute-start(f32[1,128,256]{2,1,0:T(8,128)S(1)} %get-tuple-element.30), channel_id=1, source_target_pairs={{0,16},{16,32},{32,48},{48,64},{64,80},{80,96},{96,112},{112,128},... | collective-permute-start | bytes 393224 | tf_op jit(solution)/shard_map/ppermute | solution.py:16
  6.6 6.5 %collective-permute-start = (f32[1,128,256]{2,1,0:T(8,128)S(1)}, f32[1,128,256]{2,1,0:T(8,128)S(1)}, u32[]{:S(2)}, u32[]{:S(2)}) collective-permute-start(f32[1,128,256]{2,1,0:T(8,128)S(1)} %get-tuple-element.29), channel_id=1, source_target_pairs={{16,0},{32,16},{48,32},{64,48},{80,64},{96,80},{112,96},{128,112},... | collective-permute-start | bytes 393224 | tf_op jit(solution)/shard_map/ppermute | solution.py:17
  13.1 8.1 %copy-start = (f32[8,128,256]{2,1,0:T(8,128)S(1)}, f32[8,128,256]{2,1,0:T(8,128)}, u32[]{:S(2)}) copy-start(f32[8,128,256]{2,1,0:T(8,128)} %param.3) | copy-start | bytes 3145732
  13.1 8.1 %copy-start.11 = (f32[8,128,256]{2,1,0:T(8,128)S(1)}, f32[8,128,256]{2,1,0:T(8,128)}, u32[]{:S(2)}) copy-start(f32[8,128,256]{2,1,0:T(8,128)} %param.2) | copy-start | bytes 3145732
  13.1 4.2 %collective-permute-start.3 = (f32[10,1,256]{2,1,0:T(1,128)S(1)}, f32[10,1,256]{2,1,0:T(1,128)S(1)}, u32[]{:S(2)}, u32[]{:S(2)}) collective-permute-start(f32[10,1,256]{2,1,0:T(1,128)S(1)} %get-tuple-element.23), channel_id=1, source_target_pairs={{0,1},{1,2},{2,3},{3,4},{4,5},{5,6},{6,7},{7,8},{8,9},{9,10},{10,1... | collective-permute-start | bytes 30728 | tf_op jit(solution)/shard_map/ppermute | solution.py:16
  16.0 4.4 %collective-permute-start.2 = (f32[10,1,256]{2,1,0:T(1,128)S(1)}, f32[10,1,256]{2,1,0:T(1,128)S(1)}, u32[]{:S(2)}, u32[]{:S(2)}) collective-permute-start(f32[10,1,256]{2,1,0:T(1,128)S(1)} %get-tuple-element.24), channel_id=1, source_target_pairs={{1,0},{2,1},{3,2},{4,3},{5,4},{6,5},{7,6},{8,7},{9,8},{10,9},{11,1... | collective-permute-start | bytes 30728 | tf_op jit(solution)/shard_map/ppermute | solution.py:17
  23.4 18.0 %copy-start.4 = (f32[8,128,256]{2,1,0:T(8,128)}, f32[8,128,256]{2,1,0:T(8,128)S(1)}, u32[]{:S(2)}) copy-start(f32[8,128,256]{2,1,0:T(8,128)S(1)} %get-tuple-element.13) | copy-start | bytes 3145732
  23.4 18.0 %copy-start.7 = (f32[8,128,256]{2,1,0:T(8,128)}, f32[8,128,256]{2,1,0:T(8,128)S(1)}, u32[]{:S(2)}) copy-start(f32[8,128,256]{2,1,0:T(8,128)S(1)} %get-tuple-element.15) | copy-start | bytes 3145732
  23.4 18.0 %copy-start.8 = (f32[8,128,256]{2,1,0:T(8,128)}, f32[8,128,256]{2,1,0:T(8,128)S(1)}, u32[]{:S(2)}) copy-start(f32[8,128,256]{2,1,0:T(8,128)S(1)} %get-tuple-element.16) | copy-start | bytes 3145732
  23.5 5.3 %collective-permute-start.5 = (f32[1,128,256]{2,1,0:T(8,128)S(1)}, f32[1,128,256]{2,1,0:T(8,128)S(1)}, u32[]{:S(2)}, u32[]{:S(2)}) collective-permute-start(f32[1,128,256]{2,1,0:T(8,128)S(1)} %get-tuple-element.27), channel_id=1, source_target_pairs={{0,16},{16,32},{32,48},{48,64},{64,80},{80,96},{96,112},{112,128},... | collective-permute-start | bytes 393224 | tf_op jit(solution)/shard_map/ppermute | solution.py:16
  26.8 6.3 %collective-permute-start.4 = (f32[1,128,256]{2,1,0:T(8,128)S(1)}, f32[1,128,256]{2,1,0:T(8,128)S(1)}, u32[]{:S(2)}, u32[]{:S(2)}) collective-permute-start(f32[1,128,256]{2,1,0:T(8,128)S(1)} %get-tuple-element.28), channel_id=1, source_target_pairs={{16,0},{32,16},{48,32},{64,48},{80,64},{96,80},{112,96},{128,112},... | collective-permute-start | bytes 393224 | tf_op jit(solution)/shard_map/ppermute | solution.py:17
  33.1 4.4 %collective-permute-start.7 = (f32[10,1,256]{2,1,0:T(1,128)S(1)}, f32[10,1,256]{2,1,0:T(1,128)S(1)}, u32[]{:S(2)}, u32[]{:S(2)}) collective-permute-start(f32[10,1,256]{2,1,0:T(1,128)S(1)} %get-tuple-element.21), channel_id=1, source_target_pairs={{0,1},{1,2},{2,3},{3,4},{4,5},{5,6},{6,7},{7,8},{8,9},{9,10},{10,1... | collective-permute-start | bytes 30728 | tf_op jit(solution)/shard_map/ppermute | solution.py:16
  36.3 4.4 %collective-permute-start.6 = (f32[10,1,256]{2,1,0:T(1,128)S(1)}, f32[10,1,256]{2,1,0:T(1,128)S(1)}, u32[]{:S(2)}, u32[]{:S(2)}) collective-permute-start(f32[10,1,256]{2,1,0:T(1,128)S(1)} %get-tuple-element.22), channel_id=1, source_target_pairs={{1,0},{2,1},{3,2},{4,3},{5,4},{6,5},{7,6},{8,7},{9,8},{10,9},{11,1... | collective-permute-start | bytes 30728 | tf_op jit(solution)/shard_map/ppermute | solution.py:17
  44.9 10.4 %copy-start.6 = (f32[8,128,256]{2,1,0:T(8,128)}, f32[8,128,256]{2,1,0:T(8,128)S(1)}, u32[]{:S(2)}) copy-start(f32[8,128,256]{2,1,0:T(8,128)S(1)} %get-tuple-element.11) | copy-start | bytes 3145732
  45.0 9.5 %copy-start.2 = (f32[8,128,256]{2,1,0:T(8,128)}, f32[8,128,256]{2,1,0:T(8,128)S(1)}, u32[]{:S(2)}) copy-start(f32[8,128,256]{2,1,0:T(8,128)S(1)} %mul.118) | copy-start | bytes 3145732
  45.1 5.2 %collective-permute-start.9 = (f32[1,128,256]{2,1,0:T(8,128)S(1)}, f32[1,128,256]{2,1,0:T(8,128)S(1)}, u32[]{:S(2)}, u32[]{:S(2)}) collective-permute-start(f32[1,128,256]{2,1,0:T(8,128)S(1)} %get-tuple-element.25), channel_id=1, source_target_pairs={{0,16},{16,32},{32,48},{48,64},{64,80},{80,96},{96,112},{112,128},... | collective-permute-start | bytes 393224 | tf_op jit(solution)/shard_map/ppermute | solution.py:16
  48.3 6.3 %collective-permute-start.8 = (f32[1,128,256]{2,1,0:T(8,128)S(1)}, f32[1,128,256]{2,1,0:T(8,128)S(1)}, u32[]{:S(2)}, u32[]{:S(2)}) collective-permute-start(f32[1,128,256]{2,1,0:T(8,128)S(1)} %get-tuple-element.26), channel_id=1, source_target_pairs={{16,0},{32,16},{48,32},{64,48},{80,64},{96,80},{112,96},{128,112},... | collective-permute-start | bytes 393224 | tf_op jit(solution)/shard_map/ppermute | solution.py:17
  54.6 0.7 copy-start.9
  55.2 121.2 %collective-permute-start.11 = (f32[10,1,256]{2,1,0:T(1,128)}, f32[10,1,256]{2,1,0:T(1,128)S(1)}, u32[]{:S(2)}, u32[]{:S(2)}) collective-permute-start(f32[10,1,256]{2,1,0:T(1,128)} %get-tuple-element.19), channel_id=1, source_target_pairs={{0,1},{1,2},{2,3},{3,4},{4,5},{5,6},{6,7},{7,8},{8,9},{9,10},{10,1... | collective-permute-start | bytes 30728 | tf_op jit(solution)/shard_map/ppermute | solution.py:16
  59.6 116.8 %collective-permute-start.10 = (f32[10,1,256]{2,1,0:T(1,128)}, f32[10,1,256]{2,1,0:T(1,128)S(1)}, u32[]{:S(2)}, u32[]{:S(2)}) collective-permute-start(f32[10,1,256]{2,1,0:T(1,128)} %get-tuple-element.20), channel_id=1, source_target_pairs={{1,0},{2,1},{3,2},{4,3},{5,4},{6,5},{7,6},{8,7},{9,8},{10,9},{11,1... | collective-permute-start | bytes 30728 | tf_op jit(solution)/shard_map/ppermute | solution.py:17
  176.4 2.2 copy-start.1
  176.4 2.2 copy-start.3
  176.4 2.2 copy-start.5
  176.4 2.2 copy-start.10
where the time goes:
time: 293 us; the launch traced here: 292 us
  blocking collectives  214 us (73%)
  starting transfers between devices  34.8 us (12%)
  other arithmetic  19.4 us (7%)
  waiting for transfers between devices  14.9 us (5%)
  between operations  6.86 us (2%)
    psum x2, blocking collectives, inner_pair(): return lax.psum((gamma_part, delta_part), ('gx', 'gy'))  214 us
    ppermute x6, starting transfers between devices, extended(): before = lax.ppermute(last, axis, up)  21.9 us
    ppermute x6, waiting for transfers between devices, extended(): after = lax.ppermute(initial, axis, down)  14.9 us
    ppermute x6, starting transfers between devices, extended(): after = lax.ppermute(initial, axis, down)  12.9 us
    reduce_sum x2, other arithmetic, inner_pair(): delta_part = jnp.sum(shadow * residual)  9.11 us
  transfers between devices with their start and end apart: 12, of which 4 were waited for; matrix products, arithmetic and copies ran while one was open for 0% of the time, Pallas kernels for 0%

commit v1 on v0

v1 whole, which is shorter than its diff:
```python
import functools

import jax
import jax.numpy as jnp
from jax import lax
from jax.experimental import pallas as pl
from jax.experimental.pallas import tpu as pltpu
from jax.sharding import PartitionSpec as P

MESH = pl.DeviceIdType.MESH
F32 = jnp.float32
TOP = 16


def recip(x):
    r = pl.reciprocal(x, approx=True)
    return r * (2.0 - x * r)


def fold(v):
    rows, lanes = v.shape
    out = None
    for r in range(0, rows, 8):
        for c in range(0, lanes, 128):
            piece = v[r : r + 8, c : c + 128]
            out = piece if out is None else out + piece
    return out


def kernel(sizes, source, density, t1_out, t2_out, scale_out, coef_out,
           den, src, q0, q1, inv, wx, wy, wz, msg, got_y, got_x,
           local_sem, send_sem, recv_sem, sum_send, sum_recv):
    nx, ny = sizes
    depth, width, lanes = t1_out.shape
    end = TOP + width
    last = depth - 1
    i, j = lax.axis_index("gx"), lax.axis_index("gy")
    right, left = lax.rem(i + 1, nx), lax.rem(i + nx - 1, nx)
    above, below = lax.rem(j + 1, ny), lax.rem(j + ny - 1, ny)
    row_peers = [(i, lax.rem(j + k, ny)) for k in range(1, ny)]
    col_peers = [(lax.rem(i + k, nx), j) for k in range(1, nx)]
    corners = [(a, b) for a in (right, left) for b in (above, below)]

    body, low, high = pl.ds(TOP, width), pl.ds(TOP - 8, 8), pl.ds(end, 8)
    load_d = pltpu.make_async_copy(density, den.at[pl.ds(2, depth), body], local_sem.at[0])
    load_s = pltpu.make_async_copy(source, src.at[pl.ds(1, depth), body], local_sem.at[1])
    load_d.start()
    load_s.start()

    barrier = pltpu.get_barrier_semaphore()
    everyone = row_peers + col_peers + corners
    for peer in everyone:
        pl.semaphore_signal(barrier, inc=1, device_id=peer, device_id_type=MESH)
    pl.semaphore_wait(barrier, len(everyone))

    copies = []

    def send(what, where, peer):
        k = len(copies)
        copies.append(pltpu.make_async_remote_copy(
            src_ref=what, dst_ref=where, send_sem=send_sem.at[k], recv_sem=recv_sem.at[k],
            device_id=peer, device_id_type=MESH))
        return copies[-1]

    top_rows, first_rows = pl.ds(width - 8, 8), pl.ds(0, 8)
    own_d, own_s = pl.ds(2, depth), pl.ds(1, depth)
    rim_d = [
        send(density.at[:, top_rows], den.at[own_d, low], (i, above)),
        send(density.at[:, first_rows], den.at[own_d, high], (i, below)),
    ]
    face_d = [
        send(density.at[last], den.at[1, body], (right, j)),
        send(density.at[0], den.at[depth + 2, body], (left, j)),
    ]
    rim_s = [
        send(source.at[:, top_rows], src.at[own_s, low], (i, above)),
        send(source.at[:, first_rows], src.at[own_s, high], (i, below)),
    ]
    corner_d, corner_s = [], []
    for a in (right, left):
        plane, there = (last - 1, 0) if a is right else (0, depth + 2)
        face, face_there = (last, 0) if a is right else (0, depth + 1)
        for b, rows, place in ((above, top_rows, low), (below, first_rows, high)):
            corner_d.append(send(density.at[pl.ds(plane, 2), rows], den.at[pl.ds(there, 2), place], (a, b)))
            corner_s.append(send(source.at[face, rows], src.at[face_there, place], (a, b)))
    face_s = [
        send(source.at[last], src.at[0, body], (right, j)),
        send(source.at[0], src.at[depth + 1, body], (left, j)),
    ]
    second_d = [
        send(density.at[last - 1], den.at[0, body], (right, j)),
        send(density.at[1], den.at[depth + 3, body], (left, j)),
    ]
    for copy in copies:
        copy.start()
    field = [
        send(q0.at[last - 1 + 2, body], q0.at[0, body], (right, j)),
        send(q0.at[1 + 2, body], q0.at[depth + 3, body], (left, j)),
    ]

    def arrive(group):
        for copy in group:
            copy.wait_recv()

    mids = [(r, 16) for r in range(TOP, end, 16)]
    spans = [(TOP - 8, 8)] + mids + [(end, 8)]

    def keep_y(r, v):
        if r < TOP:
            return jnp.where(j > 0, v, 0.0)
        if r >= end:
            return jnp.where(j < ny - 1, v, 0.0)
        return v

    def faces_x(p):
        for r, n in spans:
            wx[p + 2, pl.ds(r, n)] = recip(den[p + 2, pl.ds(r, n)] + den[p + 3, pl.ds(r, n)])

    def inverse(p, keep=None, rim=True):
        for r, n in spans:
            d = den[p + 2, pl.ds(r, n)]
            lane = lax.broadcasted_iota(jnp.int32, (n, lanes), 1)
            up = recip(d + den[p + 2, pl.ds(r + 1, n)])
            wy[p + 1, pl.ds(r, n)] = up
            beyond = jnp.where(lane == lanes - 1, 0.0, pltpu.roll(d, lanes - 1, 1))
            ahead = recip(d + beyond)
            wz[p + 1, pl.ds(r, n)] = jnp.where(lane == lanes - 1, 0.0, ahead)
            behind = jnp.where(lane == 0, recip(d), pltpu.roll(ahead, 1, 1))
            diag = wx[p + 2, pl.ds(r, n)] + wx[p + 1, pl.ds(r, n)]
            diag = diag + up + wy[p + 1, pl.ds(r - 1, n)] + ahead + behind
            b = recip(diag)
            inv[p + 1, pl.ds(r, n)] = b
            if rim or TOP <= r < end:
                q = keep_y(r, b * src[p + 1, pl.ds(r, n)])
                if keep is not None:
                    q = jnp.where(keep, q, 0.0)
                q0[p + 2, pl.ds(r, n)] = q

    def rim_field(p):
        for r, n in (spans[0], spans[-1]):
            q0[p + 2, pl.ds(r, n)] = keep_y(r, inv[p + 1, pl.ds(r, n)] * src[p + 1, pl.ds(r, n)])

    def coupled(v, shift, p, r, n):
        mid = v[p + shift, pl.ds(r, n)]
        total = wx[p + 2, pl.ds(r, n)] * v[p + shift + 1, pl.ds(r, n)]
        total = total + wx[p + 1, pl.ds(r, n)] * v[p + shift - 1, pl.ds(r, n)]
        total = total + wy[p + 1, pl.ds(r, n)] * v[p + shift, pl.ds(r + 1, n)]
        total = total + wy[p + 1, pl.ds(r - 1, n)] * v[p + shift, pl.ds(r - 1, n)]
        w = wz[p + 1, pl.ds(r, n)]
        total = total + w * pltpu.roll(mid, lanes - 1, 1)
        return mid, total + pltpu.roll(w * mid, 1, 1)

    def first_apply(p, sums, keep=None, own=True):
        g0, d0, ss = sums
        for r, n in spans if own else mids:
            mid, total = coupled(q0, 2, p, r, n)
            s = src[p + 1, pl.ds(r, n)]
            t = s - total
            q = keep_y(r, inv[p + 1, pl.ds(r, n)] * t)
            if keep is not None:
                q = jnp.where(keep, q, 0.0)
            q1[p + 1, pl.ds(r, n)] = q
            if own and TOP <= r < end:
                t1_out[p, pl.ds(r - TOP, n)] = t
                g0 = g0 + fold(s * mid)
                d0 = d0 + fold(t * mid)
                ss = ss + fold(t * q)
        return g0, d0, ss

    def second_apply(p, h):
        for r, n in mids:
            mid, total = coupled(q1, 1, p, r, n)
            t = t1_out[p, pl.ds(r - TOP, n)] - total
            t2_out[p, pl.ds(r - TOP, n)] = t
            h = h + fold(t * mid)
        return h

    def over(start, step, count, f, carry=None):
        def go(k, c):
            return f(start + step * k, c)
        return lax.fori_loop(0, count, go, carry)

    def plain(f):
        def g(p, c):
            f(p)
            return c
        return g

    zero = jnp.zeros((8, 128), F32)
    load_d.wait()
    over(0, 1, last, plain(lambda p: [
        wx.__setitem__((p + 2, pl.ds(r, n)), recip(den[p + 2, pl.ds(r, n)] + den[p + 3, pl.ds(r, n)])) for r, n in mids]), 0)
    load_s.wait()
    arrive(rim_d)

    @pl.when(j == 0)
    def _():
        den[2 : depth + 2, TOP - 8 : TOP] = jnp.zeros((depth, 8, lanes), F32)

    @pl.when(j == ny - 1)
    def _():
        den[2 : depth + 2, end : end + 8] = jnp.zeros((depth, 8, lanes), F32)

    over(0, 1, last, plain(lambda p: [
        wx.__setitem__((p + 2, pl.ds(r, n)), recip(den[p + 2, pl.ds(r, n)] + den[p + 3, pl.ds(r, n)])) for r, n in (spans[0], spans[-1])]), 0)
    over(1, last - 2, 2, plain(lambda p: inverse(p, rim=False)), 0)
    for copy in field:
        copy.start()
    over(2, 1, depth - 4, plain(lambda p: inverse(p, rim=False)), 0)
    arrive(rim_s)
    over(1, 1, depth - 2, plain(rim_field), 0)
    sums = over(2, 1, depth - 4, first_apply, (zero, zero, zero))

    arrive(face_d)
    arrive(corner_d)
    for edge, first, there in ((0, i == 0, 0), (nx - 1, i == nx - 1, depth + 2)):
        @pl.when(first)
        def _():
            near = there + 1 if edge == 0 else there
            den[near, TOP - 8 : end + 8] = jnp.zeros((width + 16, lanes), F32)
    for bound, first, rows in ((0, j == 0, TOP - 8), (ny - 1, j == ny - 1, end)):
        @pl.when(first)
        def _():
            den[0:2, rows : rows + 8] = jnp.zeros((2, 8, lanes), F32)
            den[depth + 2 : depth + 4, rows : rows + 8] = jnp.zeros((2, 8, lanes), F32)

    over(-1, depth, 2, plain(faces_x), 0)
    arrive(corner_s)
    over(0, last, 2, plain(inverse), 0)
    sums = over(1, last - 2, 2, first_apply, sums)

    arrive(face_s)
    arrive(second_d)
    over(-2, depth + 2, 2, plain(faces_x), 0)

    def outer(p):
        return jnp.logical_or(jnp.logical_and(p < 0, i > 0), jnp.logical_and(p > 0, i < nx - 1))

    over(-1, depth + 1, 2, plain(lambda p: inverse(p, keep=outer(p))), 0)
    g0, d0, ss = over(0, last, 2, first_apply, sums)
    h = over(1, 1, depth - 2, second_apply, zero)

    arrive(field)
    over(-1, depth + 1, 2, plain(lambda p: first_apply(p, (None,) * 3, keep=outer(p), own=False)), 0)
    h = over(0, last, 2, second_apply, h)

    group = lax.broadcasted_iota(jnp.int32, (1, 128), 1) // 32
    row = jnp.zeros((1, 128), F32)
    for k, part in enumerate((g0, d0, ss, h)):
        v = jnp.sum(part, axis=0, keepdims=True)
        v = v + pltpu.roll(v, 64, 1)
        v = v + pltpu.roll(v, 32, 1)
        row = jnp.where(group == k, v, row)

    def spread(k, value, peers, got):
        msg[k] = value
        for s, peer in enumerate(peers):
            pltpu.make_async_remote_copy(
                src_ref=msg.at[k], dst_ref=got.at[s], send_sem=sum_send.at[k], recv_sem=sum_recv.at[k],
                device_id=peer, device_id_type=MESH).start()

    def gathered(k, value, got):
        pltpu.make_async_copy(got, got, sum_recv.at[k]).wait()
        for s in range(got.shape[0]):
            value = value + got[s]
        return value

    spread(0, row, row_peers, got_y)

    def scales(p):
        for r, n in mids:
            half = 0.5 * inv[p + 1, pl.ds(r, n)]
            scale_out[p, pl.ds(r - TOP, n)] = half * lax.rsqrt(half)

    over(0, 1, depth, plain(scales), 0)
    row = gathered(0, row, got_y)
    spread(1, row, col_peers, got_x)
    for copy in copies:
        copy.wait_send()
    row = gathered(1, row, got_x)
    pltpu.make_async_copy(got_y, got_y, sum_send.at[0]).wait()
    pltpu.make_async_copy(got_x, got_x, sum_send.at[1]).wait()

    def total(k):
        return jnp.broadcast_to(jnp.sum(jnp.where(group == k, row, 0.0), axis=1, keepdims=True), (1, 128))

    g0, d0, ss, h = (total(k) for k in range(4))
    alpha0 = g0 / d0
    gamma1 = g0 - 2.0 * alpha0 * d0 + alpha0 * alpha0 * ss
    delta1 = d0 - 2.0 * alpha0 * ss + alpha0 * alpha0 * h
    beta1 = gamma1 / g0
    alpha1 = gamma1 / (delta1 - beta1 * gamma1 / alpha0)
    coef_out[0:1] = alpha0 + alpha1 * (1.0 + beta1)
    coef_out[1:2] = alpha0 * alpha1


def solution(mesh):
    sizes = (mesh.shape["gx"], mesh.shape["gy"])

    def shards(source, density):
        depth, width, lanes = source.shape
        shape = jax.ShapeDtypeStruct(source.shape, F32)

        def planes(n):
            return pltpu.VMEM((n, TOP + width + 16, lanes), F32)

        vmem = pl.BlockSpec(memory_space=pltpu.VMEM)
        t1, t2, scale, coef = pl.pallas_call(
            functools.partial(kernel, sizes),
            out_shape=(shape, shape, shape, jax.ShapeDtypeStruct((2, 128), F32)),
            in_specs=[pl.BlockSpec(memory_space=pltpu.HBM)] * 2,
            out_specs=(vmem,) * 4,
            scratch_shapes=[
                planes(depth + 4), planes(depth + 2), planes(depth + 4), planes(depth + 2),
                planes(depth + 2), planes(depth + 3), planes(depth + 2), planes(depth + 2),
                pltpu.VMEM((2, 1, 128), F32),
                pltpu.VMEM((sizes[1] - 1, 1, 128), F32),
                pltpu.VMEM((sizes[0] - 1, 1, 128), F32),
                pltpu.SemaphoreType.DMA((2,)),
                pltpu.SemaphoreType.DMA((20,)),
                pltpu.SemaphoreType.DMA((20,)),
                pltpu.SemaphoreType.DMA((2,)),
                pltpu.SemaphoreType.DMA((2,)),
            ],
            compiler_params=pltpu.CompilerParams(
                collective_id=1, has_side_effects=True, vmem_limit_bytes=36 * 1024 * 1024),
        )(source, density)
        a, b = coef[0, 0], coef[1, 0]
        pressure = scale * scale * (a * source - b * t1)
        residual = scale * (source - a * t1 + b * t2)
        return pressure, residual

    spec = P("gx", "gy", None)
    return jax.shard_map(shards, mesh=mesh, in_specs=(spec, spec), out_specs=(spec, spec), check_vma=False)
```

time: 293 us -> 46.6 us (0.16)
  blocking collectives: 214 us -> 0 us
  Pallas kernels: 0 us -> 39.9 us
  starting transfers between devices: 34.8 us -> 0 us
  other arithmetic: 19.4 us -> 2.86 us
  waiting for transfers between devices: 14.9 us -> 0 us
  between operations: 6.86 us -> 0.65 us
    psum x2 -> x0, blocking collectives: 214 us -> none  [inner_pair(): return lax.psum((gamma_part, delta_part), ('gx', 'gy'))]
    pallas_call x0 -> x1, Pallas kernels: none -> 39.9 us  [shards(): pl.pallas_call(functools.partial(kernel, sizes), out_shape=(shape, shape,...]
    ppermute x12 -> x0, starting transfers between devices: 34.8 us -> none  [the longest x6 21.9 us: extended(): before = lax.ppermute(last, axis, up)]
    ppermute x12 -> x0, waiting for transfers between devices: 14.9 us -> none  [the longest x6 14.9 us: extended(): after = lax.ppermute(initial, axis, down)]
    reduce_sum x2 -> x0, other arithmetic: 9.11 us -> none  [inner_pair(): delta_part = jnp.sum(shadow * residual)]
    concatenate x5 -> x0, other arithmetic: 4.3 us -> none  [extended(): shard = jnp.concatenate([before, shard, after], axis=dim)]
    sub x1 -> x0, other arithmetic: 3.59 us -> none  [shards(): residual = residual - alpha_now * along]
  transfers between devices with their start and end apart: 12 -> 0, of which waited for: 4 -> 0; matrix products, arithmetic and copies ran while one was open for 0% -> 0% of each run, Pallas kernels for 0% -> 0%
where the time goes in v1:
time: 46.6 us; the launch traced here: 46.3 us
  Pallas kernels  39.9 us (86%)
  local copies, waits for them, and re-layouts  2.97 us (6%)
  other arithmetic  2.86 us (6%)
  between operations  0.65 us (1%)
    pallas_call x1, Pallas kernels, shards(): pl.pallas_call(functools.partial(kernel, sizes), out_shape=(shape, shape,...  39.9 us
    mul x1, other arithmetic, shards(): residual = scale * (source - a * t1 + b * t2)  2.86 us
    unnamed x4, local copies, waits for them, and re-layouts  2.44 us

profile of v1, /device:TPU:1, one launch (start us, length us, event | category | flops | bytes accessed | tf_op | source)
XLA Modules:
  0.0 46.3 jit_solution(13508646755835013461)
XLA Ops:
  0.6 0.0 copy-start
  0.6 1.2 %copy-done = f32[8,128,256]{2,1,0:T(8,128)S(1)} copy-done((f32[8,128,256]{2,1,0:T(8,128)S(1)}, f32[8,128,256]{2,1,0:T(8,128)}, u32[]{:S(2)}) %copy-start) | copy-done | bytes 1048600
  1.9 0.0 copy-start.1
  1.9 1.2 %copy-done.1 = f32[8,128,256]{2,1,0:T(8,128)S(1)} copy-done((f32[8,128,256]{2,1,0:T(8,128)S(1)}, f32[8,128,256]{2,1,0:T(8,128)}, u32[]{:S(2)}) %copy-start.1) | copy-done | bytes 1048600
  3.1 39.9 %shard_map.41 = (f32[8,128,256]{2,1,0:T(8,128)S(1)}, f32[8,128,256]{2,1,0:T(8,128)S(1)}, f32[8,128,256]{2,1,0:T(8,128)S(1)}, f32[2,128]{1,0:T(2,128)S(1)}) custom-call(f32[8,128,256]{2,1,0:T(8,128)S(1)} %copy-done, f32[8,128,256]{2,1,0:T(8,128)S(1)} %copy-done.1), custom_call_target="tpu_custom_call" | custom-call | tf_op jit(solution)/shard_map/pallas_call | solution.py:308
  43.0 0.5 %fusion = (f32[1,1]{1,0:T(1,128)}, f32[1,1]{1,0:T(1,128)}) fusion(f32[2,128]{1,0:T(2,128)S(1)} %get-tuple-element.7), kind=kLoop, calls=%fused_computation.2 | loop fusion | bytes 16 | tf_op jit(solution)/shard_map/slice | solution.py:328
  43.5 2.9 %add_multiply_fusion = (f32[8,128,256]{2,1,0:T(8,128)}, f32[8,128,256]{2,1,0:T(8,128)}) fusion(f32[8,128,256]{2,1,0:T(8,128)S(1)} %get-tuple-element.6, f32[8,128,256]{2,1,0:T(8,128)S(1)} %get-tuple-element.9, f32[8,128,256]{2,1,0:T(8,128)S(1)} %copy-done, f32[8,128,256]{2,1,0:T(8,128)S(1)} %get-tuple-element.8, f32[]{:T(128)} %bitcast.1, f32[]{:T(128)} %bitcast), kind=kLoop, calls=%fused_computation | loop fusion | flops 2621440 | bytes 6291464 | tf_op jit(solution)/shard_map/mul | solution.py:330
Async XLA Ops:
  0.6 1.2 %copy-start = (f32[8,128,256]{2,1,0:T(8,128)S(1)}, f32[8,128,256]{2,1,0:T(8,128)}, u32[]{:S(2)}) copy-start(f32[8,128,256]{2,1,0:T(8,128)} %source.1) | copy-start | bytes 3145732
  1.9 1.2 %copy-start.1 = (f32[8,128,256]{2,1,0:T(8,128)S(1)}, f32[8,128,256]{2,1,0:T(8,128)}, u32[]{:S(2)}) copy-start(f32[8,128,256]{2,1,0:T(8,128)} %density.1) | copy-start | bytes 3145732

commit v2 on v1

--- a/solution.py
+++ b/solution.py
@@ -27,7 +27,7 @@
     return out
 
 
-def kernel(sizes, source, density, t1_out, t2_out, scale_out, coef_out,
+def kernel(sizes, source, density, t0_out, t1_out, t2_out, scale_out, coef_out,
            den, src, q0, q1, inv, wx, wy, wz, msg, got_y, got_x,
            local_sem, send_sem, recv_sem, sum_send, sum_recv):
     nx, ny = sizes
@@ -112,8 +112,8 @@
             return jnp.where(j < ny - 1, v, 0.0)
         return v
 
-    def faces_x(p):
-        for r, n in spans:
+    def faces_x(p, rows=spans):
+        for r, n in rows:
             wx[p + 2, pl.ds(r, n)] = recip(den[p + 2, pl.ds(r, n)] + den[p + 3, pl.ds(r, n)])
 
     def inverse(p, keep=None, rim=True):
@@ -188,8 +188,7 @@
 
     zero = jnp.zeros((8, 128), F32)
     load_d.wait()
-    over(0, 1, last, plain(lambda p: [
-        wx.__setitem__((p + 2, pl.ds(r, n)), recip(den[p + 2, pl.ds(r, n)] + den[p + 3, pl.ds(r, n)])) for r, n in mids]), 0)
+    over(0, 1, last, plain(lambda p: faces_x(p, mids)), 0)
     load_s.wait()
     arrive(rim_d)
 
@@ -201,8 +200,7 @@
     def _():
         den[2 : depth + 2, end : end + 8] = jnp.zeros((depth, 8, lanes), F32)
 
-    over(0, 1, last, plain(lambda p: [
-        wx.__setitem__((p + 2, pl.ds(r, n)), recip(den[p + 2, pl.ds(r, n)] + den[p + 3, pl.ds(r, n)])) for r, n in (spans[0], spans[-1])]), 0)
+    over(0, 1, last, plain(lambda p: faces_x(p, (spans[0], spans[-1]))), 0)
     over(1, last - 2, 2, plain(lambda p: inverse(p, rim=False)), 0)
     for copy in field:
         copy.start()
@@ -269,8 +267,13 @@
 
     def scales(p):
         for r, n in mids:
+            rows = pl.ds(r - TOP, n)
             half = 0.5 * inv[p + 1, pl.ds(r, n)]
-            scale_out[p, pl.ds(r - TOP, n)] = half * lax.rsqrt(half)
+            scale = half * lax.rsqrt(half)
+            scale_out[p, rows] = scale
+            t0_out[p, rows] = scale * src[p + 1, pl.ds(r, n)]
+            t1_out[p, rows] = scale * t1_out[p, rows]
+            t2_out[p, rows] = scale * t2_out[p, rows]
 
     over(0, 1, depth, plain(scales), 0)
     row = gathered(0, row, got_y)
@@ -294,6 +297,20 @@
     coef_out[1:2] = alpha0 * alpha1
 
 
+def combine(t0, t1, t2, scale, coef, pressure, residual, held_p, held_r, sem):
+    a, b = coef[0:1, 0:1], coef[1:2, 0:1]
+    copies = []
+    for p in range(t0.shape[0]):
+        u0, u1 = t0[p], t1[p]
+        held_p[p] = scale[p] * (a * u0 - b * u1)
+        held_r[p] = u0 - a * u1 + b * t2[p]
+        for k, (held, out) in enumerate(((held_p, pressure), (held_r, residual))):
+            copies.append(pltpu.make_async_copy(held.at[p], out.at[p], sem.at[k, p]))
+            copies[-1].start()
+    for copy in copies:
+        copy.wait()
+
+
 def solution(mesh):
     sizes = (mesh.shape["gx"], mesh.shape["gy"])
 
@@ -305,11 +322,12 @@
             return pltpu.VMEM((n, TOP + width + 16, lanes), F32)
 
         vmem = pl.BlockSpec(memory_space=pltpu.VMEM)
-        t1, t2, scale, coef = pl.pallas_call(
+        hbm = pl.BlockSpec(memory_space=pltpu.HBM)
+        t0, t1, t2, scale, coef = pl.pallas_call(
             functools.partial(kernel, sizes),
-            out_shape=(shape, shape, shape, jax.ShapeDtypeStruct((2, 128), F32)),
-            in_specs=[pl.BlockSpec(memory_space=pltpu.HBM)] * 2,
-            out_specs=(vmem,) * 4,
+            out_shape=(shape,) * 4 + (jax.ShapeDtypeStruct((2, 128), F32),),
+            in_specs=[hbm] * 2,
+            out_specs=(vmem,) * 5,
             scratch_shapes=[
                 planes(depth + 4), planes(depth + 2), planes(depth + 4), planes(depth + 2),
                 planes(depth + 2), planes(depth + 3), planes(depth + 2), planes(depth + 2),
@@ -324,10 +342,16 @@
             ],
             compiler_params=pltpu.CompilerParams(
                 collective_id=1, has_side_effects=True, vmem_limit_bytes=36 * 1024 * 1024),
-        )(source, density)
-        a, b = coef[0, 0], coef[1, 0]
-        pressure = scale * scale * (a * source - b * t1)
-        residual = scale * (source - a * t1 + b * t2)
+        )(pltpu.with_memory_space_constraint(source, pltpu.HBM), pltpu.with_memory_space_constraint(density, pltpu.HBM))
+        pressure, residual = pl.pallas_call(
+            combine,
+            out_shape=(shape, shape),
+            in_specs=[vmem] * 5,
+            out_specs=(hbm, hbm),
+            scratch_shapes=[
+                pltpu.VMEM(source.shape, F32), pltpu.VMEM(source.shape, F32), pltpu.SemaphoreType.DMA((2, depth))],
+            compiler_params=pltpu.CompilerParams(vmem_limit_bytes=16 * 1024 * 1024),
+        )(t0, t1, t2, scale, coef)
         return pressure, residual
 
     spec = P("gx", "gy", None)

time: 46.6 us -> 42.2 us (0.906)
  local copies, waits for them, and re-layouts: 2.97 us -> 0 us
  other arithmetic: 2.86 us -> 0 us
  Pallas kernels: 39.9 us -> 41.5 us
    mul x1 -> x0, other arithmetic: 2.86 us -> none  [shards(): residual = scale * (source - a * t1 + b * t2)]
    unnamed x4 -> x0, local copies, waits for them, and re-layouts: 2.44 us -> none
    pallas_call x1 -> x2, Pallas kernels: 39.9 us -> 41.5 us  [the longest x1 40 us: shards(): pl.pallas_call(functools.partial(kernel, sizes), out_shape=(shape,) * 4 +...]
    slice x1 -> x0, local copies, waits for them, and re-layouts: 0.52 us -> none  [shards(): a, b = (coef[0, 0], coef[1, 0])]
where the time goes in v2:
time: 42.2 us; the launch traced here: 42.1 us
  Pallas kernels  41.5 us (98%)
  between operations  0.64 us (2%)
    pallas_call x1, Pallas kernels, shards(): pl.pallas_call(functools.partial(kernel, sizes), out_shape=(shape,) * 4 +...  40 us
    pallas_call x1, Pallas kernels, shards(): pl.pallas_call(combine, out_shape=(shape, shape), in_specs=[vmem] * 5, ou...  1.5 us

profile of v2, /device:TPU:1, one launch (start us, length us, event | category | flops | bytes accessed | tf_op | source)
XLA Modules:
  0.0 42.1 jit_solution(16819445019135387739)
XLA Ops:
  0.6 40.0 %shard_map.41 = (f32[8,128,256]{2,1,0:T(8,128)S(1)}, f32[8,128,256]{2,1,0:T(8,128)S(1)}, f32[8,128,256]{2,1,0:T(8,128)S(1)}, f32[8,128,256]{2,1,0:T(8,128)S(1)}, f32[2,128]{1,0:T(2,128)S(1)}) custom-call(f32[8,128,256]{2,1,0:T(8,128)} %source.1, f32[8,128,256]{2,1,0:T(8,128)} %density.1), custom_call_target="tpu_custom_call" | custom-call | tf_op jit(solution)/shard_map/pallas_call | solution.py:326
  40.6 1.5 %shard_map.42 = (f32[8,128,256]{2,1,0:T(8,128)}, f32[8,128,256]{2,1,0:T(8,128)}) custom-call(f32[8,128,256]{2,1,0:T(8,128)S(1)} %get-tuple-element.7.t0, f32[8,128,256]{2,1,0:T(8,128)S(1)} %get-tuple-element.8.t1, f32[8,128,256]{2,1,0:T(8,128)S(1)} %get-tuple-element.9.t2, f32[8,128,256]{2,1,0:T(8,128)S(1)} %get-tuple-element.10.scale, ...), custom_call_target="tpu_custom_call" | custom-call | tf_op jit(solution)/shard_map/pallas_call | solution.py:346

commit v3 on v2

--- a/solution.py
+++ b/solution.py
@@ -29,7 +29,7 @@
 
 def kernel(sizes, source, density, t0_out, t1_out, t2_out, scale_out, coef_out,
            den, src, q0, q1, inv, wx, wy, wz, msg, got_y, got_x,
-           local_sem, send_sem, recv_sem, sum_send, sum_recv):
+           local_sem, send_sem, recv_sem, sum_send, sum_recv, known):
     nx, ny = sizes
     depth, width, lanes = t1_out.shape
     end = TOP + width
@@ -48,10 +48,21 @@
     load_s.start()
 
     barrier = pltpu.get_barrier_semaphore()
-    everyone = row_peers + col_peers + corners
-    for peer in everyone:
+    rounds = (nx - 1).bit_length() - 1
+    nearby = [(right, j), (left, j)] + corners + row_peers
+    for peer in nearby:
         pl.semaphore_signal(barrier, inc=1, device_id=peer, device_id_type=MESH)
-    pl.semaphore_wait(barrier, len(everyone))
+    pl.semaphore_wait(barrier, len(nearby))
+
+    def tell(k):
+        if k >= rounds:
+            return
+        for step in (2**k, nx - 2**k):
+            pl.semaphore_signal(known.at[k], inc=1, device_id=(lax.rem(i + step, nx), j), device_id_type=MESH)
+
+    def heard(k):
+        if k < rounds:
+            pl.semaphore_wait(known.at[k], 2)
 
     copies = []
 
@@ -187,6 +198,7 @@
         return g
 
     zero = jnp.zeros((8, 128), F32)
+    tell(0)
     load_d.wait()
     over(0, 1, last, plain(lambda p: faces_x(p, mids)), 0)
     load_s.wait()
@@ -204,11 +216,15 @@
     over(1, last - 2, 2, plain(lambda p: inverse(p, rim=False)), 0)
     for copy in field:
         copy.start()
+    heard(0)
+    tell(1)
     over(2, 1, depth - 4, plain(lambda p: inverse(p, rim=False)), 0)
     arrive(rim_s)
     over(1, 1, depth - 2, plain(rim_field), 0)
     sums = over(2, 1, depth - 4, first_apply, (zero, zero, zero))
 
+    heard(1)
+    tell(2)
     arrive(face_d)
     arrive(corner_d)
     for edge, first, there in ((0, i == 0, 0), (nx - 1, i == nx - 1, depth + 2)):
@@ -227,6 +243,8 @@
     over(0, last, 2, plain(inverse), 0)
     sums = over(1, last - 2, 2, first_apply, sums)
 
+    heard(2)
+    tell(3)
     arrive(face_s)
     arrive(second_d)
     over(-2, depth + 2, 2, plain(faces_x), 0)
@@ -277,6 +295,7 @@
 
     over(0, 1, depth, plain(scales), 0)
     row = gathered(0, row, got_y)
+    heard(3)
     spread(1, row, col_peers, got_x)
     for copy in copies:
         copy.wait_send()
@@ -339,6 +358,7 @@
                 pltpu.SemaphoreType.DMA((20,)),
                 pltpu.SemaphoreType.DMA((2,)),
                 pltpu.SemaphoreType.DMA((2,)),
+                pltpu.SemaphoreType.REGULAR((4,)),
             ],
             compiler_params=pltpu.CompilerParams(
                 collective_id=1, has_side_effects=True, vmem_limit_bytes=36 * 1024 * 1024),

time: 42.2 us -> 41.9 us (level)
  no operation moved by 1% of the time
where the time goes in v3:
time: 41.9 us; the launch traced here: 41.8 us
  Pallas kernels  41.1 us (98%)
  between operations  0.64 us (2%)
    pallas_call x1, Pallas kernels, shards(): pl.pallas_call(functools.partial(kernel, sizes), out_shape=(shape,) * 4 +...  39.6 us
    pallas_call x1, Pallas kernels, shards(): pl.pallas_call(combine, out_shape=(shape, shape), in_specs=[vmem] * 5, ou...  1.5 us

profile of v3, /device:TPU:1, one launch (start us, length us, event | category | flops | bytes accessed | tf_op | source)
XLA Modules:
  0.0 41.8 jit_solution(10303629708563031409)
XLA Ops:
  0.6 39.6 %shard_map.41 = (f32[8,128,256]{2,1,0:T(8,128)S(1)}, f32[8,128,256]{2,1,0:T(8,128)S(1)}, f32[8,128,256]{2,1,0:T(8,128)S(1)}, f32[8,128,256]{2,1,0:T(8,128)S(1)}, f32[2,128]{1,0:T(2,128)S(1)}) custom-call(f32[8,128,256]{2,1,0:T(8,128)} %source.1, f32[8,128,256]{2,1,0:T(8,128)} %density.1), custom_call_target="tpu_custom_call" | custom-call | tf_op jit(solution)/shard_map/pallas_call | solution.py:345
  40.3 1.5 %shard_map.42 = (f32[8,128,256]{2,1,0:T(8,128)}, f32[8,128,256]{2,1,0:T(8,128)}) custom-call(f32[8,128,256]{2,1,0:T(8,128)S(1)} %get-tuple-element.7.t0, f32[8,128,256]{2,1,0:T(8,128)S(1)} %get-tuple-element.8.t1, f32[8,128,256]{2,1,0:T(8,128)S(1)} %get-tuple-element.9.t2, f32[8,128,256]{2,1,0:T(8,128)S(1)} %get-tuple-element.10.scale, ...), custom_call_target="tpu_custom_call" | custom-call | tf_op jit(solution)/shard_map/pallas_call | solution.py:366

commit v4 on v2

--- a/solution.py
+++ b/solution.py
@@ -29,17 +29,37 @@
 
 def kernel(sizes, source, density, t0_out, t1_out, t2_out, scale_out, coef_out,
            den, src, q0, q1, inv, wx, wy, wz, msg, got_y, got_x,
-           local_sem, send_sem, recv_sem, sum_send, sum_recv):
+           local_sem, send_sem, recv_sem, sum_send, sum_recv, known):
     nx, ny = sizes
     depth, width, lanes = t1_out.shape
     end = TOP + width
     last = depth - 1
     i, j = lax.axis_index("gx"), lax.axis_index("gy")
-    right, left = lax.rem(i + 1, nx), lax.rem(i + nx - 1, nx)
-    above, below = lax.rem(j + 1, ny), lax.rem(j + ny - 1, ny)
-    row_peers = [(i, lax.rem(j + k, ny)) for k in range(1, ny)]
-    col_peers = [(lax.rem(i + k, nx), j) for k in range(1, nx)]
-    corners = [(a, b) for a in (right, left) for b in (above, below)]
+    right, left = (i + 1, i < nx - 1, i > 0), (i - 1, i > 0, i < nx - 1)
+    above, below = (j + 1, j < ny - 1, j > 0), (j - 1, j > 0, j < ny - 1)
+
+    def beside(a, b):
+        both = jnp.logical_and
+        return ((a[0], b[0]), both(a[1], b[1]), both(a[2], b[2]))
+
+    sides = [((right[0], j), right[1], right[2]), ((left[0], j), left[1], left[2])]
+    side = int(ny**0.5)
+    chips = nx // 2
+    core = lax.rem(i, 2)
+
+    def far(k, n):
+        return min(k, n - k)
+
+    offsets = [(b, a, c) for b in range(side) for a in range(side) for c in range(2)][1:]
+    offsets.sort(key=lambda o: -far(o[0], side) - far(o[1], side))
+    row_peers = [
+        (i + c * (1 - 2 * core), lax.rem(j // side + b, side) * side + lax.rem(lax.rem(j, side) + a, side))
+        for b, a, c in offsets
+    ]
+    col_peers = [
+        (lax.rem(i + 2 * k, nx), j) for k in sorted(range(1, chips), key=lambda k: -far(k, chips))
+    ]
+    corners = [beside(a, b) for a in (right, left) for b in (above, below)]
 
     body, low, high = pl.ds(TOP, width), pl.ds(TOP - 8, 8), pl.ds(end, 8)
     load_d = pltpu.make_async_copy(density, den.at[pl.ds(2, depth), body], local_sem.at[0])
@@ -48,59 +68,81 @@
     load_s.start()
 
     barrier = pltpu.get_barrier_semaphore()
-    everyone = row_peers + col_peers + corners
-    for peer in everyone:
+    for peer in row_peers + [(lax.rem(i + 2, nx), j), (lax.rem(i + nx - 2, nx), j)]:
         pl.semaphore_signal(barrier, inc=1, device_id=peer, device_id_type=MESH)
-    pl.semaphore_wait(barrier, len(everyone))
+    across = i + 2 * core - 1
+    inside = jnp.logical_and(across >= 0, across < nx)
+    for row, there in ((j, True), (j + 1, j < ny - 1), (j - 1, j > 0)):
+        @pl.when(jnp.logical_and(inside, there))
+        def _():
+            pl.semaphore_signal(barrier, inc=1, device_id=(across, row), device_id_type=MESH)
+    beside_y = (j > 0).astype(jnp.int32) + (j < ny - 1).astype(jnp.int32)
+    pl.semaphore_wait(barrier, len(row_peers) + 2 + inside.astype(jnp.int32) * (1 + beside_y))
+
+    rounds = (chips - 1).bit_length() - 1
+
+    def tell(k):
+        if k < rounds:
+            for step in (2 ** (k + 1), nx - 2 ** (k + 1)):
+                pl.semaphore_signal(
+                    known.at[k], inc=1, device_id=(lax.rem(i + step, nx), j), device_id_type=MESH)
+
+    def heard(k):
+        if k < rounds:
+            pl.semaphore_wait(known.at[k], 2)
 
     copies = []
 
     def send(what, where, peer):
         k = len(copies)
-        copies.append(pltpu.make_async_remote_copy(
+        who, there, opposite = peer
+        copies.append((pltpu.make_async_remote_copy(
             src_ref=what, dst_ref=where, send_sem=send_sem.at[k], recv_sem=recv_sem.at[k],
-            device_id=peer, device_id_type=MESH))
+            device_id=who, device_id_type=MESH), there, opposite))
         return copies[-1]
+
+    def begin(group):
+        for copy, there, _ in group:
+            pl.when(there)(copy.start)
 
     top_rows, first_rows = pl.ds(width - 8, 8), pl.ds(0, 8)
     own_d, own_s = pl.ds(2, depth), pl.ds(1, depth)
     rim_d = [
-        send(density.at[:, top_rows], den.at[own_d, low], (i, above)),
-        send(density.at[:, first_rows], den.at[own_d, high], (i, below)),
+        send(density.at[:, top_rows], den.at[own_d, low], ((i, above[0]), above[1], above[2])),
+        send(density.at[:, first_rows], den.at[own_d, high], ((i, below[0]), below[1], below[2])),
     ]
     face_d = [
-        send(density.at[last], den.at[1, body], (right, j)),
-        send(density.at[0], den.at[depth + 2, body], (left, j)),
+        send(density.at[last], den.at[1, body], sides[0]),
+        send(density.at[0], den.at[depth + 2, body], sides[1]),
     ]
     rim_s = [
-        send(source.at[:, top_rows], src.at[own_s, low], (i, above)),
-        send(source.at[:, first_rows], src.at[own_s, high], (i, below)),
+        send(source.at[:, top_rows], src.at[own_s, low], ((i, above[0]), above[1], above[2])),
+        send(source.at[:, first_rows], src.at[own_s, high], ((i, below[0]), below[1], below[2])),
     ]
     corner_d, corner_s = [], []
     for a in (right, left):
         plane, there = (last - 1, 0) if a is right else (0, depth + 2)
         face, face_there = (last, 0) if a is right else (0, depth + 1)
         for b, rows, place in ((above, top_rows, low), (below, first_rows, high)):
-            corner_d.append(send(density.at[pl.ds(plane, 2), rows], den.at[pl.ds(there, 2), place], (a, b)))
-            corner_s.append(send(source.at[face, rows], src.at[face_there, place], (a, b)))
+            corner_d.append(send(density.at[pl.ds(plane, 2), rows], den.at[pl.ds(there, 2), place], beside(a, b)))
+            corner_s.append(send(source.at[face, rows], src.at[face_there, place], beside(a, b)))
     face_s = [
-        send(source.at[last], src.at[0, body], (right, j)),
-        send(source.at[0], src.at[depth + 1, body], (left, j)),
+        send(source.at[last], src.at[0, body], sides[0]),
+        send(source.at[0], src.at[depth + 1, body], sides[1]),
     ]
     second_d = [
-        send(density.at[last - 1], den.at[0, body], (right, j)),
-        send(density.at[1], den.at[depth + 3, body], (left, j)),
-    ]
-    for copy in copies:
-        copy.start()
+        send(density.at[last - 1], den.at[0, body], sides[0]),
+        send(density.at[1], den.at[depth + 3, body], sides[1]),
+    ]
+    begin(copies)
     field = [
-        send(q0.at[last - 1 + 2, body], q0.at[0, body], (right, j)),
-        send(q0.at[1 + 2, body], q0.at[depth + 3, body], (left, j)),
+        send(q0.at[last - 1 + 2, body], q0.at[0, body], sides[0]),
+        send(q0.at[1 + 2, body], q0.at[depth + 3, body], sides[1]),
     ]
 
     def arrive(group):
-        for copy in group:
-            copy.wait_recv()
+        for copy, _, opposite in group:
+            pl.when(opposite)(copy.wait_recv)
 
     mids = [(r, 16) for r in range(TOP, end, 16)]
     spans = [(TOP - 8, 8)] + mids + [(end, 8)]
@@ -187,9 +229,12 @@
         return g
 
     zero = jnp.zeros((8, 128), F32)
+    tell(0)
     load_d.wait()
     over(0, 1, last, plain(lambda p: faces_x(p, mids)), 0)
     load_s.wait()
+    heard(0)
+    tell(1)
     arrive(rim_d)
 
     @pl.when(j == 0)
@@ -202,9 +247,10 @@
 
     over(0, 1, last, plain(lambda p: faces_x(p, (spans[0], spans[-1]))), 0)
     over(1, last - 2, 2, plain(lambda p: inverse(p, rim=False)), 0)
-    for copy in field:
-        copy.start()
+    begin(field)
     over(2, 1, depth - 4, plain(lambda p: inverse(p, rim=False)), 0)
+    heard(1)
+    tell(2)
     arrive(rim_s)
     over(1, 1, depth - 2, plain(rim_field), 0)
     sums = over(2, 1, depth - 4, first_apply, (zero, zero, zero))
@@ -277,9 +323,10 @@
 
     over(0, 1, depth, plain(scales), 0)
     row = gathered(0, row, got_y)
+    heard(2)
     spread(1, row, col_peers, got_x)
-    for copy in copies:
-        copy.wait_send()
+    for copy, there, _ in copies:
+        pl.when(there)(copy.wait_send)
     row = gathered(1, row, got_x)
     pltpu.make_async_copy(got_y, got_y, sum_send.at[0]).wait()
     pltpu.make_async_copy(got_x, got_x, sum_send.at[1]).wait()
@@ -332,13 +379,14 @@
                 planes(depth + 4), planes(depth + 2), planes(depth + 4), planes(depth + 2),
                 planes(depth + 2), planes(depth + 3), planes(depth + 2), planes(depth + 2),
                 pltpu.VMEM((2, 1, 128), F32),
-                pltpu.VMEM((sizes[1] - 1, 1, 128), F32),
-                pltpu.VMEM((sizes[0] - 1, 1, 128), F32),
+                pltpu.VMEM((2 * sizes[1] - 1, 1, 128), F32),
+                pltpu.VMEM((sizes[0] // 2 - 1, 1, 128), F32),
                 pltpu.SemaphoreType.DMA((2,)),
                 pltpu.SemaphoreType.DMA((20,)),
                 pltpu.SemaphoreType.DMA((20,)),
                 pltpu.SemaphoreType.DMA((2,)),
                 pltpu.SemaphoreType.DMA((2,)),
+                pltpu.SemaphoreType.REGULAR((3,)),
             ],
             compiler_params=pltpu.CompilerParams(
                 collective_id=1, has_side_effects=True, vmem_limit_bytes=36 * 1024 * 1024),

time: 42.2 us -> 39.5 us (0.936)
  Pallas kernels: 41.5 us -> 38.7 us
    pallas_call x1, Pallas kernels: 40 us -> 37.2 us  [shards(): pl.pallas_call(functools.partial(kernel, sizes), out_shape=(shape,) * 4 +...]
where the time goes in v4:
time: 39.5 us; the launch traced here: 39.3 us
  Pallas kernels  38.7 us (98%)
  between operations  0.64 us (2%)
    pallas_call x1, Pallas kernels, shards(): pl.pallas_call(functools.partial(kernel, sizes), out_shape=(shape,) * 4 +...  37.2 us
    pallas_call x1, Pallas kernels, shards(): pl.pallas_call(combine, out_shape=(shape, shape), in_specs=[vmem] * 5, ou...  1.5 us

profile of v4, /device:TPU:1, one launch (start us, length us, event | category | flops | bytes accessed | tf_op | source)
XLA Modules:
  0.0 39.3 jit_solution(4245505440955013874)
XLA Ops:
  0.6 37.2 %shard_map.41 = (f32[8,128,256]{2,1,0:T(8,128)S(1)}, f32[8,128,256]{2,1,0:T(8,128)S(1)}, f32[8,128,256]{2,1,0:T(8,128)S(1)}, f32[8,128,256]{2,1,0:T(8,128)S(1)}, f32[2,128]{1,0:T(2,128)S(1)}) custom-call(f32[8,128,256]{2,1,0:T(8,128)} %source.1, f32[8,128,256]{2,1,0:T(8,128)} %density.1), custom_call_target="tpu_custom_call" | custom-call | tf_op jit(solution)/shard_map/pallas_call | solution.py:373
  37.8 1.5 %shard_map.42 = (f32[8,128,256]{2,1,0:T(8,128)}, f32[8,128,256]{2,1,0:T(8,128)}) custom-call(f32[8,128,256]{2,1,0:T(8,128)S(1)} %get-tuple-element.7.t0, f32[8,128,256]{2,1,0:T(8,128)S(1)} %get-tuple-element.8.t1, f32[8,128,256]{2,1,0:T(8,128)S(1)} %get-tuple-element.9.t2, f32[8,128,256]{2,1,0:T(8,128)S(1)} %get-tuple-element.10.scale, ...), custom_call_target="tpu_custom_call" | custom-call | tf_op jit(solution)/shard_map/pallas_call | solution.py:394

commit v5 on v4

--- a/solution.py
+++ b/solution.py
@@ -68,16 +68,15 @@
     load_s.start()
 
     barrier = pltpu.get_barrier_semaphore()
-    for peer in row_peers + [(lax.rem(i + 2, nx), j), (lax.rem(i + nx - 2, nx), j)]:
-        pl.semaphore_signal(barrier, inc=1, device_id=peer, device_id_type=MESH)
     across = i + 2 * core - 1
     inside = jnp.logical_and(across >= 0, across < nx)
     for row, there in ((j, True), (j + 1, j < ny - 1), (j - 1, j > 0)):
         @pl.when(jnp.logical_and(inside, there))
         def _():
             pl.semaphore_signal(barrier, inc=1, device_id=(across, row), device_id_type=MESH)
+    for peer in [(lax.rem(i + 2, nx), j), (lax.rem(i + nx - 2, nx), j)] + row_peers[::-1]:
+        pl.semaphore_signal(barrier, inc=1, device_id=peer, device_id_type=MESH)
     beside_y = (j > 0).astype(jnp.int32) + (j < ny - 1).astype(jnp.int32)
-    pl.semaphore_wait(barrier, len(row_peers) + 2 + inside.astype(jnp.int32) * (1 + beside_y))
 
     rounds = (chips - 1).bit_length() - 1
 
@@ -90,55 +89,6 @@
     def heard(k):
         if k < rounds:
             pl.semaphore_wait(known.at[k], 2)
-
-    copies = []
-
-    def send(what, where, peer):
-        k = len(copies)
-        who, there, opposite = peer
-        copies.append((pltpu.make_async_remote_copy(
-            src_ref=what, dst_ref=where, send_sem=send_sem.at[k], recv_sem=recv_sem.at[k],
-            device_id=who, device_id_type=MESH), there, opposite))
-        return copies[-1]
-
-    def begin(group):
-        for copy, there, _ in group:
-            pl.when(there)(copy.start)
-
-    top_rows, first_rows = pl.ds(width - 8, 8), pl.ds(0, 8)
-    own_d, own_s = pl.ds(2, depth), pl.ds(1, depth)
-    rim_d = [
-        send(density.at[:, top_rows], den.at[own_d, low], ((i, above[0]), above[1], above[2])),
-        send(density.at[:, first_rows], den.at[own_d, high], ((i, below[0]), below[1], below[2])),
-    ]
-    face_d = [
-        send(density.at[last], den.at[1, body], sides[0]),
-        send(density.at[0], den.at[depth + 2, body], sides[1]),
-    ]
-    rim_s = [
-        send(source.at[:, top_rows], src.at[own_s, low], ((i, above[0]), above[1], above[2])),
-        send(source.at[:, first_rows], src.at[own_s, high], ((i, below[0]), below[1], below[2])),
-    ]
-    corner_d, corner_s = [], []
-    for a in (right, left):
-        plane, there = (last - 1, 0) if a is right else (0, depth + 2)
-        face, face_there = (last, 0) if a is right else (0, depth + 1)
-        for b, rows, place in ((above, top_rows, low), (below, first_rows, high)):
-            corner_d.append(send(density.at[pl.ds(plane, 2), rows], den.at[pl.ds(there, 2), place], beside(a, b)))
-            corner_s.append(send(source.at[face, rows], src.at[face_there, place], beside(a, b)))
-    face_s = [
-        send(source.at[last], src.at[0, body], sides[0]),
-        send(source.at[0], src.at[depth + 1, body], sides[1]),
-    ]
-    second_d = [
-        send(density.at[last - 1], den.at[0, body], sides[0]),
-        send(density.at[1], den.at[depth + 3, body], sides[1]),
-    ]
-    begin(copies)
-    field = [
-        send(q0.at[last - 1 + 2, body], q0.at[0, body], sides[0]),
-        send(q0.at[1 + 2, body], q0.at[depth + 3, body], sides[1]),
-    ]
 
     def arrive(group):
         for copy, _, opposite in group:
@@ -158,18 +108,20 @@
         for r, n in rows:
             wx[p + 2, pl.ds(r, n)] = recip(den[p + 2, pl.ds(r, n)] + den[p + 3, pl.ds(r, n)])
 
-    def inverse(p, keep=None, rim=True):
-        for r, n in spans:
+    def faces_y(p, rows=spans):
+        for r, n in rows:
+            wy[p + 1, pl.ds(r, n)] = recip(den[p + 2, pl.ds(r, n)] + den[p + 2, pl.ds(r + 1, n)])
+
+    def inverse(p, rows=spans, keep=None, rim=True):
+        for r, n in rows:
             d = den[p + 2, pl.ds(r, n)]
             lane = lax.broadcasted_iota(jnp.int32, (n, lanes), 1)
-            up = recip(d + den[p + 2, pl.ds(r + 1, n)])
-            wy[p + 1, pl.ds(r, n)] = up
             beyond = jnp.where(lane == lanes - 1, 0.0, pltpu.roll(d, lanes - 1, 1))
             ahead = recip(d + beyond)
             wz[p + 1, pl.ds(r, n)] = jnp.where(lane == lanes - 1, 0.0, ahead)
             behind = jnp.where(lane == 0, recip(d), pltpu.roll(ahead, 1, 1))
             diag = wx[p + 2, pl.ds(r, n)] + wx[p + 1, pl.ds(r, n)]
-            diag = diag + up + wy[p + 1, pl.ds(r - 1, n)] + ahead + behind
+            diag = diag + wy[p + 1, pl.ds(r, n)] + wy[p + 1, pl.ds(r - 1, n)] + ahead + behind
             b = recip(diag)
             inv[p + 1, pl.ds(r, n)] = b
             if rim or TOP <= r < end:
@@ -177,6 +129,10 @@
                 if keep is not None:
                     q = jnp.where(keep, q, 0.0)
                 q0[p + 2, pl.ds(r, n)] = q
+
+    def whole(p, keep=None):
+        faces_y(p)
+        inverse(p, spans, keep)
 
     def rim_field(p):
         for r, n in (spans[0], spans[-1]):
@@ -192,9 +148,9 @@
         total = total + w * pltpu.roll(mid, lanes - 1, 1)
         return mid, total + pltpu.roll(w * mid, 1, 1)
 
-    def first_apply(p, sums, keep=None, own=True):
+    def first_apply(p, sums, rows=spans, keep=None, own=True):
         g0, d0, ss = sums
-        for r, n in spans if own else mids:
+        for r, n in rows:
             mid, total = coupled(q0, 2, p, r, n)
             s = src[p + 1, pl.ds(r, n)]
             t = s - total
@@ -228,13 +184,64 @@
             return c
         return g
 
+    copies = []
+
+    def send(what, where, peer):
+        k = len(copies)
+        who, there, opposite = peer
+        copies.append((pltpu.make_async_remote_copy(
+            src_ref=what, dst_ref=where, send_sem=send_sem.at[k], recv_sem=recv_sem.at[k],
+            device_id=who, device_id_type=MESH), there, opposite))
+        return copies[-1]
+
+    def begin(group):
+        for copy, there, _ in group:
+            pl.when(there)(copy.start)
+
+    own_d, own_s = pl.ds(2, depth), pl.ds(1, depth)
+
+    def ends(n):
+        return ((above, pl.ds(width - n, n), pl.ds(TOP - n, n)), (below, pl.ds(0, n), pl.ds(end, n)))
+
+    rim_d = [send(density.at[:, rows], den.at[own_d, place], ((i, b[0]), b[1], b[2])) for b, rows, place in ends(3)]
+    face_d = [
+        send(density.at[last], den.at[1, body], sides[0]),
+        send(density.at[0], den.at[depth + 2, body], sides[1]),
+    ]
+    rim_s = [send(source.at[:, rows], src.at[own_s, place], ((i, b[0]), b[1], b[2])) for b, rows, place in ends(2)]
+    corner_d, corner_s = [], []
+    for a in (right, left):
+        plane, there = (last - 1, 0) if a is right else (0, depth + 2)
+        face, face_there = (last, 0) if a is right else (0, depth + 1)
+        for b, rows, place in ends(2):
+            corner_d.append(send(density.at[pl.ds(plane, 2), rows], den.at[pl.ds(there, 2), place], beside(a, b)))
+        for b, rows, place in ends(1):
+            corner_s.append(send(source.at[face, rows], src.at[face_there, place], beside(a, b)))
+    face_s = [
+        send(source.at[last], src.at[0, body], sides[0]),
+        send(source.at[0], src.at[depth + 1, body], sides[1]),
+    ]
+    second_d = [
+        send(density.at[last - 1], den.at[0, body], sides[0]),
+        send(density.at[1], den.at[depth + 3, body], sides[1]),
+    ]
+    load_d.wait()
+    over(0, 1, last, plain(lambda p: faces_x(p, mids)), 0)
+    over(1, 1, depth - 2, plain(lambda p: faces_y(p, mids[:-1])), 0)
+    pl.semaphore_wait(barrier, len(row_peers) + 2 + inside.astype(jnp.int32) * (1 + beside_y))
+    begin(copies)
+    field = [
+        send(q0.at[last - 1 + 2, body], q0.at[0, body], sides[0]),
+        send(q0.at[1 + 2, body], q0.at[depth + 3, body], sides[1]),
+    ]
+
     zero = jnp.zeros((8, 128), F32)
     tell(0)
-    load_d.wait()
-    over(0, 1, last, plain(lambda p: faces_x(p, mids)), 0)
     load_s.wait()
+    over(1, 1, depth - 2, plain(lambda p: inverse(p, mids[1:-1])), 0)
     heard(0)
     tell(1)
+    sums = over(2, 1, depth - 4, lambda p, c: first_apply(p, c, mids[2:-2]), (zero, zero, zero))
     arrive(rim_d)
 
     @pl.when(j == 0)
@@ -245,15 +252,19 @@
     def _():
         den[2 : depth + 2, end : end + 8] = jnp.zeros((depth, 8, lanes), F32)
 
+    def rims(p):
+        faces_y(p, (spans[0], spans[-2], spans[-1]))
+        inverse(p, spans[:2] + spans[-2:], rim=False)
+
     over(0, 1, last, plain(lambda p: faces_x(p, (spans[0], spans[-1]))), 0)
-    over(1, last - 2, 2, plain(lambda p: inverse(p, rim=False)), 0)
+    over(1, last - 2, 2, plain(rims), 0)
     begin(field)
-    over(2, 1, depth - 4, plain(lambda p: inverse(p, rim=False)), 0)
+    over(2, 1, depth - 4, plain(rims), 0)
     heard(1)
     tell(2)
     arrive(rim_s)
     over(1, 1, depth - 2, plain(rim_field), 0)
-    sums = over(2, 1, depth - 4, first_apply, (zero, zero, zero))
+    sums = over(2, 1, depth - 4, lambda p, c: first_apply(p, c, spans[:3] + spans[-3:]), sums)
 
     arrive(face_d)
     arrive(corner_d)
@@ -270,7 +281,7 @@
 
     over(-1, depth, 2, plain(faces_x), 0)
     arrive(corner_s)
-    over(0, last, 2, plain(inverse), 0)
+    over(0, last, 2, plain(whole), 0)
     sums = over(1, last - 2, 2, first_apply, sums)
 
     arrive(face_s)
@@ -280,12 +291,12 @@
     def outer(p):
         return jnp.logical_or(jnp.logical_and(p < 0, i > 0), jnp.logical_and(p > 0, i < nx - 1))
 
-    over(-1, depth + 1, 2, plain(lambda p: inverse(p, keep=outer(p))), 0)
+    over(-1, depth + 1, 2, plain(lambda p: whole(p, outer(p))), 0)
     g0, d0, ss = over(0, last, 2, first_apply, sums)
     h = over(1, 1, depth - 2, second_apply, zero)
 
     arrive(field)
-    over(-1, depth + 1, 2, plain(lambda p: first_apply(p, (None,) * 3, keep=outer(p), own=False)), 0)
+    over(-1, depth + 1, 2, plain(lambda p: first_apply(p, (None,) * 3, mids, outer(p), False)), 0)
     h = over(0, last, 2, second_apply, h)
 
     group = lax.broadcasted_iota(jnp.int32, (1, 128), 1) // 32

time: 39.5 us -> 38.2 us (0.967)
  Pallas kernels: 38.7 us -> 37.4 us
    pallas_call x1, Pallas kernels: 37.2 us -> 35.9 us  [shards(): pl.pallas_call(functools.partial(kernel, sizes), out_shape=(shape,) * 4 +...]
where the time goes in v5:
time: 38.2 us; the launch traced here: 38 us
  Pallas kernels  37.4 us (98%)
  between operations  0.64 us (2%)
    pallas_call x1, Pallas kernels, shards(): pl.pallas_call(functools.partial(kernel, sizes), out_shape=(shape,) * 4 +...  35.9 us
    pallas_call x1, Pallas kernels, shards(): pl.pallas_call(combine, out_shape=(shape, shape), in_specs=[vmem] * 5, ou...  1.5 us

profile of v5, /device:TPU:1, one launch (start us, length us, event | category | flops | bytes accessed | tf_op | source)
XLA Modules:
  0.0 38.0 jit_solution(14499381158215936215)
XLA Ops:
  0.6 35.9 %shard_map.41 = (f32[8,128,256]{2,1,0:T(8,128)S(1)}, f32[8,128,256]{2,1,0:T(8,128)S(1)}, f32[8,128,256]{2,1,0:T(8,128)S(1)}, f32[8,128,256]{2,1,0:T(8,128)S(1)}, f32[2,128]{1,0:T(2,128)S(1)}) custom-call(f32[8,128,256]{2,1,0:T(8,128)} %source.1, f32[8,128,256]{2,1,0:T(8,128)} %density.1), custom_call_target="tpu_custom_call" | custom-call | tf_op jit(solution)/shard_map/pallas_call | solution.py:384
  36.5 1.5 %shard_map.42 = (f32[8,128,256]{2,1,0:T(8,128)}, f32[8,128,256]{2,1,0:T(8,128)}) custom-call(f32[8,128,256]{2,1,0:T(8,128)S(1)} %get-tuple-element.7.t0, f32[8,128,256]{2,1,0:T(8,128)S(1)} %get-tuple-element.8.t1, f32[8,128,256]{2,1,0:T(8,128)S(1)} %get-tuple-element.9.t2, f32[8,128,256]{2,1,0:T(8,128)S(1)} %get-tuple-element.10.scale, ...), custom_call_target="tpu_custom_call" | custom-call | tf_op jit(solution)/shard_map/pallas_call | solution.py:405

commit v6 on v5

--- a/solution.py
+++ b/solution.py
@@ -112,53 +112,49 @@
         for r, n in rows:
             wy[p + 1, pl.ds(r, n)] = recip(den[p + 2, pl.ds(r, n)] + den[p + 2, pl.ds(r + 1, n)])
 
-    def inverse(p, rows=spans, keep=None, rim=True):
+    def in_plane_faces(p, r, n):
+        d = den[p + 2, pl.ds(r, n)]
+        lane = lax.broadcasted_iota(jnp.int32, (n, lanes), 1)
+        beyond = jnp.where(lane == lanes - 1, 0.0, pltpu.roll(d, lanes - 1, 1))
+        ahead = recip(d + beyond)
+        wz[p + 1, pl.ds(r, n)] = jnp.where(lane == lanes - 1, 0.0, ahead)
+        behind = jnp.where(lane == 0, recip(d), pltpu.roll(ahead, 1, 1))
+        return wy[p + 1, pl.ds(r, n)] + wy[p + 1, pl.ds(r - 1, n)] + ahead + behind
+
+    def inverse(p, rows=spans, rim=True):
         for r, n in rows:
-            d = den[p + 2, pl.ds(r, n)]
-            lane = lax.broadcasted_iota(jnp.int32, (n, lanes), 1)
-            beyond = jnp.where(lane == lanes - 1, 0.0, pltpu.roll(d, lanes - 1, 1))
-            ahead = recip(d + beyond)
-            wz[p + 1, pl.ds(r, n)] = jnp.where(lane == lanes - 1, 0.0, ahead)
-            behind = jnp.where(lane == 0, recip(d), pltpu.roll(ahead, 1, 1))
-            diag = wx[p + 2, pl.ds(r, n)] + wx[p + 1, pl.ds(r, n)]
-            diag = diag + wy[p + 1, pl.ds(r, n)] + wy[p + 1, pl.ds(r - 1, n)] + ahead + behind
+            diag = in_plane_faces(p, r, n) + wx[p + 2, pl.ds(r, n)] + wx[p + 1, pl.ds(r, n)]
             b = recip(diag)
             inv[p + 1, pl.ds(r, n)] = b
             if rim or TOP <= r < end:
-                q = keep_y(r, b * src[p + 1, pl.ds(r, n)])
-                if keep is not None:
-                    q = jnp.where(keep, q, 0.0)
-                q0[p + 2, pl.ds(r, n)] = q
-
-    def whole(p, keep=None):
-        faces_y(p)
-        inverse(p, spans, keep)
+                q0[p + 2, pl.ds(r, n)] = keep_y(r, b * src[p + 1, pl.ds(r, n)])
 
     def rim_field(p):
         for r, n in (spans[0], spans[-1]):
             q0[p + 2, pl.ds(r, n)] = keep_y(r, inv[p + 1, pl.ds(r, n)] * src[p + 1, pl.ds(r, n)])
 
-    def coupled(v, shift, p, r, n):
+    def in_plane(v, shift, p, r, n):
         mid = v[p + shift, pl.ds(r, n)]
-        total = wx[p + 2, pl.ds(r, n)] * v[p + shift + 1, pl.ds(r, n)]
-        total = total + wx[p + 1, pl.ds(r, n)] * v[p + shift - 1, pl.ds(r, n)]
-        total = total + wy[p + 1, pl.ds(r, n)] * v[p + shift, pl.ds(r + 1, n)]
+        total = wy[p + 1, pl.ds(r, n)] * v[p + shift, pl.ds(r + 1, n)]
         total = total + wy[p + 1, pl.ds(r - 1, n)] * v[p + shift, pl.ds(r - 1, n)]
         w = wz[p + 1, pl.ds(r, n)]
         total = total + w * pltpu.roll(mid, lanes - 1, 1)
         return mid, total + pltpu.roll(w * mid, 1, 1)
 
-    def first_apply(p, sums, rows=spans, keep=None, own=True):
+    def coupled(v, shift, p, r, n):
+        mid, total = in_plane(v, shift, p, r, n)
+        total = total + wx[p + 2, pl.ds(r, n)] * v[p + shift + 1, pl.ds(r, n)]
+        return mid, total + wx[p + 1, pl.ds(r, n)] * v[p + shift - 1, pl.ds(r, n)]
+
+    def first_apply(p, sums, rows=spans):
         g0, d0, ss = sums
         for r, n in rows:
             mid, total = coupled(q0, 2, p, r, n)
             s = src[p + 1, pl.ds(r, n)]
             t = s - total
             q = keep_y(r, inv[p + 1, pl.ds(r, n)] * t)
-            if keep is not None:
-                q = jnp.where(keep, q, 0.0)
             q1[p + 1, pl.ds(r, n)] = q
-            if own and TOP <= r < end:
+            if TOP <= r < end:
                 t1_out[p, pl.ds(r - TOP, n)] = t
                 g0 = g0 + fold(s * mid)
                 d0 = d0 + fold(t * mid)
@@ -171,6 +167,86 @@
             t = t1_out[p, pl.ds(r - TOP, n)] - total
             t2_out[p, pl.ds(r - TOP, n)] = t
             h = h + fold(t * mid)
+        return h
+
+    def at_end(k):
+        return depth * k + k - 1, last * k, 1 + (last - 2) * k, 1 + depth * k, (depth + 2) * k, 2 + (last - 1) * k
+
+    def beyond_of(k):
+        return (depth + 3) * k
+
+    def present(k):
+        return jnp.where(k == 0, i, nx - 1 - i) > 0
+
+    def own_weights(k):
+        _, own, _, _, _, inner = at_end(k)
+        faces_y(own)
+        for r, n in spans:
+            inv[own + 1, pl.ds(r, n)] = in_plane_faces(own, r, n) + wx[inner, pl.ds(r, n)]
+
+    def own_field(k):
+        out, own, _, face, _, _ = at_end(k)
+        for r, n in spans:
+            rows = pl.ds(r, n)
+            w = recip(den[out + 2, rows] + den[own + 2, rows])
+            wx[face, rows] = w
+            b = recip(inv[own + 1, rows] + w)
+            inv[own + 1, rows] = b
+            q0[own + 2, rows] = keep_y(r, b * src[own + 1, rows])
+
+    def end_weights(k):
+        out, own, nxt, face, _, inner = at_end(k)
+        faces_y(out)
+        for r, n in spans:
+            rows = pl.ds(r, n)
+            inv[out + 1, rows] = in_plane_faces(out, r, n) + wx[face, rows]
+            mid, total = in_plane(q0, 2, own, r, n)
+            q1[own + 1, rows] = src[own + 1, rows] - total - wx[inner, rows] * q0[nxt + 2, rows]
+
+    def end_field(k, sums):
+        out, own, _, face, outer, _ = at_end(k)
+        g0, d0, ss = sums
+        for r, n in spans:
+            rows = pl.ds(r, n)
+            w = recip(den[out + 2, rows] + den[beyond_of(k), rows])
+            wx[outer, rows] = w
+            b = recip(inv[out + 1, rows] + w)
+            inv[out + 1, rows] = b
+            q = jnp.where(present(k), keep_y(r, b * src[out + 1, rows]), 0.0)
+            q0[out + 2, rows] = q
+            t = q1[own + 1, rows] - wx[face, rows] * q
+            q = keep_y(r, inv[own + 1, rows] * t)
+            q1[own + 1, rows] = q
+            if TOP <= r < end:
+                s, mid = src[own + 1, rows], q0[own + 2, rows]
+                t1_out[own, pl.ds(r - TOP, n)] = t
+                g0 = g0 + fold(s * mid)
+                d0 = d0 + fold(t * mid)
+                ss = ss + fold(t * q)
+        return g0, d0, ss
+
+    def end_second(k, h):
+        out, own, nxt, face, _, inner = at_end(k)
+        for r, n in mids:
+            rows = pl.ds(r, n)
+            _, total = in_plane(q0, 2, out, r, n)
+            q1[out + 1, rows] = src[out + 1, rows] - total - wx[face, rows] * q0[own + 2, rows]
+            mid, total = in_plane(q1, 1, own, r, n)
+            t = t1_out[own, pl.ds(r - TOP, n)] - total - wx[inner, rows] * q1[nxt + 1, rows]
+            t2_out[own, pl.ds(r - TOP, n)] = t
+            h = h + fold(t * mid)
+        return h
+
+    def end_last(k, rows_of, h):
+        out, own, _, face, outer, _ = at_end(k)
+        for r, n in rows_of:
+            rows = pl.ds(r, n)
+            t = q1[out + 1, rows] - wx[outer, rows] * q0[beyond_of(k), rows]
+            q = jnp.where(present(k), inv[out + 1, rows] * t, 0.0)
+            c = wx[face, rows] * q
+            t2_out[own, pl.ds(r - TOP, n)] = t2_out[own, pl.ds(r - TOP, n)] - c
+            if h is not None:
+                h = h - 2.0 * fold(c * q1[own + 1, rows])
         return h
 
     def over(start, step, count, f, carry=None):
@@ -230,10 +306,15 @@
     over(1, 1, depth - 2, plain(lambda p: faces_y(p, mids[:-1])), 0)
     pl.semaphore_wait(barrier, len(row_peers) + 2 + inside.astype(jnp.int32) * (1 + beside_y))
     begin(copies)
-    field = [
-        send(q0.at[last - 1 + 2, body], q0.at[0, body], sides[0]),
-        send(q0.at[1 + 2, body], q0.at[depth + 3, body], sides[1]),
-    ]
+    half = width // 2
+    lower, upper = pl.ds(TOP, half), pl.ds(TOP + half, half)
+    field, field_later = (
+        [
+            send(q0.at[last + 1, a], q0.at[0, a], sides[0]),
+            send(q0.at[3, b], q0.at[depth + 3, b], sides[1]),
+        ]
+        for a, b in ((upper, lower), (lower, upper))
+    )
 
     zero = jnp.zeros((8, 128), F32)
     tell(0)
@@ -259,6 +340,7 @@
     over(0, 1, last, plain(lambda p: faces_x(p, (spans[0], spans[-1]))), 0)
     over(1, last - 2, 2, plain(rims), 0)
     begin(field)
+    begin(field_later)
     over(2, 1, depth - 4, plain(rims), 0)
     heard(1)
     tell(2)
@@ -266,6 +348,8 @@
     over(1, 1, depth - 2, plain(rim_field), 0)
     sums = over(2, 1, depth - 4, lambda p, c: first_apply(p, c, spans[:3] + spans[-3:]), sums)
 
+    over(0, 1, 2, plain(own_weights), 0)
+    h = over(3, 1, depth - 6, second_apply, zero)
     arrive(face_d)
     arrive(corner_d)
     for edge, first, there in ((0, i == 0, 0), (nx - 1, i == nx - 1, depth + 2)):
@@ -279,25 +363,21 @@
             den[0:2, rows : rows + 8] = jnp.zeros((2, 8, lanes), F32)
             den[depth + 2 : depth + 4, rows : rows + 8] = jnp.zeros((2, 8, lanes), F32)
 
-    over(-1, depth, 2, plain(faces_x), 0)
     arrive(corner_s)
-    over(0, last, 2, plain(whole), 0)
+    over(0, 1, 2, plain(own_field), 0)
     sums = over(1, last - 2, 2, first_apply, sums)
+    over(0, 1, 2, plain(end_weights), 0)
+    h = over(2, depth - 5, 2, second_apply, h)
 
     arrive(face_s)
     arrive(second_d)
-    over(-2, depth + 2, 2, plain(faces_x), 0)
-
-    def outer(p):
-        return jnp.logical_or(jnp.logical_and(p < 0, i > 0), jnp.logical_and(p > 0, i < nx - 1))
-
-    over(-1, depth + 1, 2, plain(lambda p: whole(p, outer(p))), 0)
-    g0, d0, ss = over(0, last, 2, first_apply, sums)
-    h = over(1, 1, depth - 2, second_apply, zero)
+    g0, d0, ss = over(0, 1, 2, end_field, sums)
+    h = over(0, 1, 2, end_second, h)
+    h = over(1, last - 2, 2, second_apply, h)
 
     arrive(field)
-    over(-1, depth + 1, 2, plain(lambda p: first_apply(p, (None,) * 3, mids, outer(p), False)), 0)
-    h = over(0, last, 2, second_apply, h)
+    low_half, high_half = mids[: half // 16], mids[half // 16 :]
+    h = end_last(1, low_half, end_last(0, high_half, h))
 
     group = lax.broadcasted_iota(jnp.int32, (1, 128), 1) // 32
     row = jnp.zeros((1, 128), F32)
@@ -332,6 +412,9 @@
             t1_out[p, rows] = scale * t1_out[p, rows]
             t2_out[p, rows] = scale * t2_out[p, rows]
 
+    arrive(field_later)
+    end_last(0, low_half, None)
+    end_last(1, high_half, None)
     over(0, 1, depth, plain(scales), 0)
     row = gathered(0, row, got_y)
     heard(2)
@@ -393,8 +476,8 @@
                 pltpu.VMEM((2 * sizes[1] - 1, 1, 128), F32),
                 pltpu.VMEM((sizes[0] // 2 - 1, 1, 128), F32),
                 pltpu.SemaphoreType.DMA((2,)),
-                pltpu.SemaphoreType.DMA((20,)),
-                pltpu.SemaphoreType.DMA((20,)),
+                pltpu.SemaphoreType.DMA((22,)),
+                pltpu.SemaphoreType.DMA((22,)),
                 pltpu.SemaphoreType.DMA((2,)),
                 pltpu.SemaphoreType.DMA((2,)),
                 pltpu.SemaphoreType.REGULAR((3,)),

time: 38.2 us -> 38.1 us (level)
  no operation moved by 1% of the time
where the time goes in v6:
time: 38.1 us; the launch traced here: 37.9 us
  Pallas kernels  37.3 us (98%)
  between operations  0.64 us (2%)
    pallas_call x1, Pallas kernels, shards(): pl.pallas_call(functools.partial(kernel, sizes), out_shape=(shape,) * 4 +...  35.8 us
    pallas_call x1, Pallas kernels, shards(): pl.pallas_call(combine, out_shape=(shape, shape), in_specs=[vmem] * 5, ou...  1.5 us

profile of v6, /device:TPU:1, one launch (start us, length us, event | category | flops | bytes accessed | tf_op | source)
XLA Modules:
  0.0 37.9 jit_solution(2086561734517591481)
XLA Ops:
  0.6 35.8 %shard_map.41 = (f32[8,128,256]{2,1,0:T(8,128)S(1)}, f32[8,128,256]{2,1,0:T(8,128)S(1)}, f32[8,128,256]{2,1,0:T(8,128)S(1)}, f32[8,128,256]{2,1,0:T(8,128)S(1)}, f32[2,128]{1,0:T(2,128)S(1)}) custom-call(f32[8,128,256]{2,1,0:T(8,128)} %source.1, f32[8,128,256]{2,1,0:T(8,128)} %density.1), custom_call_target="tpu_custom_call" | custom-call | tf_op jit(solution)/shard_map/pallas_call | solution.py:467
  36.4 1.5 %shard_map.42 = (f32[8,128,256]{2,1,0:T(8,128)}, f32[8,128,256]{2,1,0:T(8,128)}) custom-call(f32[8,128,256]{2,1,0:T(8,128)S(1)} %get-tuple-element.7.t0, f32[8,128,256]{2,1,0:T(8,128)S(1)} %get-tuple-element.8.t1, f32[8,128,256]{2,1,0:T(8,128)S(1)} %get-tuple-element.9.t2, f32[8,128,256]{2,1,0:T(8,128)S(1)} %get-tuple-element.10.scale, ...), custom_call_target="tpu_custom_call" | custom-call | tf_op jit(solution)/shard_map/pallas_call | solution.py:488

commit v7 on v6

--- a/solution.py
+++ b/solution.py
@@ -305,7 +305,7 @@
     over(0, 1, last, plain(lambda p: faces_x(p, mids)), 0)
     over(1, 1, depth - 2, plain(lambda p: faces_y(p, mids[:-1])), 0)
     pl.semaphore_wait(barrier, len(row_peers) + 2 + inside.astype(jnp.int32) * (1 + beside_y))
-    begin(copies)
+    begin(rim_d + rim_s + corner_d + corner_s + face_d + face_s + second_d)
     half = width // 2
     lower, upper = pl.ds(TOP, half), pl.ds(TOP + half, half)
     field, field_later = (

time: 38.1 us -> 38.1 us (level)
  no operation moved by 1% of the time
where the time goes in v7:
time: 38.1 us; the launch traced here: 38 us
  Pallas kernels  37.3 us (98%)
  between operations  0.64 us (2%)
    pallas_call x1, Pallas kernels, shards(): pl.pallas_call(functools.partial(kernel, sizes), out_shape=(shape,) * 4 +...  35.8 us
    pallas_call x1, Pallas kernels, shards(): pl.pallas_call(combine, out_shape=(shape, shape), in_specs=[vmem] * 5, ou...  1.5 us

profile of v7, /device:TPU:1, one launch (start us, length us, event | category | flops | bytes accessed | tf_op | source)
XLA Modules:
  0.0 38.0 jit_solution(9486661918512031995)
XLA Ops:
  0.6 35.8 %shard_map.41 = (f32[8,128,256]{2,1,0:T(8,128)S(1)}, f32[8,128,256]{2,1,0:T(8,128)S(1)}, f32[8,128,256]{2,1,0:T(8,128)S(1)}, f32[8,128,256]{2,1,0:T(8,128)S(1)}, f32[2,128]{1,0:T(2,128)S(1)}) custom-call(f32[8,128,256]{2,1,0:T(8,128)} %source.1, f32[8,128,256]{2,1,0:T(8,128)} %density.1), custom_call_target="tpu_custom_call" | custom-call | tf_op jit(solution)/shard_map/pallas_call | solution.py:467
  36.5 1.5 %shard_map.42 = (f32[8,128,256]{2,1,0:T(8,128)}, f32[8,128,256]{2,1,0:T(8,128)}) custom-call(f32[8,128,256]{2,1,0:T(8,128)S(1)} %get-tuple-element.7.t0, f32[8,128,256]{2,1,0:T(8,128)S(1)} %get-tuple-element.8.t1, f32[8,128,256]{2,1,0:T(8,128)S(1)} %get-tuple-element.9.t2, f32[8,128,256]{2,1,0:T(8,128)S(1)} %get-tuple-element.10.scale, ...), custom_call_target="tpu_custom_call" | custom-call | tf_op jit(solution)/shard_map/pallas_call | solution.py:488
